TPU v7x, 32 devices: a whole 2x2x4 slice. The times are simulated.
32 devices in a mesh: dp: 16 (over z, x, core), fsdp: 2 (over y).
Axes of the slice: x: 2, y: 2, z: 4, core: 2. Of those that a mesh axis runs over, the one named last changes fastest.
Arguments:
- block_input: bfloat16 [3, 32, 64, 64, 192], P(None, 'dp', 'fsdp'), may hold values from -12 to 12
- embedding: bfloat16 [3, 32, 768], P(None, 'dp'), may hold values from -6 to 6
- out_cotangent: bfloat16 [3, 32, 64, 64, 192], P(None, 'dp', 'fsdp'), may hold values from -6 to 6
- conv_weights: bfloat16 [3, 2, 3, 3, 192, 192], P(None, None, None, None, 'fsdp'), may hold values from -0.15625 to 0.15625
- affine_weight: bfloat16 [3, 768, 384], P(None, 'fsdp'), may hold values from -0.21875 to 0.21875
- gains: bfloat16 [3, 2, 192], P(None, None, 'fsdp'), may hold values from 0.5 to 1.5
- biases: bfloat16 [3, 6, 192], P(None, None, 'fsdp'), may hold values from -2 to 2
- counts: int32 [16], P('dp'), may hold values from 0 to 2, as said below
Outputs:
- block_output: bfloat16 [3, 32, 64, 64, 192], P(None, 'dp', 'fsdp')
- input_grad: bfloat16 [3, 32, 64, 64, 192], P(None, 'dp', 'fsdp')
- conv_grads: float32 [2, 2, 3, 3, 192, 192], P(None, None, None, None, 'fsdp')
- affine_grad: float32 [2, 768, 384], P(None, 'fsdp')
- gain_grads: float32 [2, 2, 192], P(None, None, 'fsdp')
- bias_grads: float32 [2, 6, 192], P(None, None, 'fsdp')
Inputs may be any that keep to these rules, and one draw needn't show every extreme that they name: `counts`: some index of dp holds 2 images and some holds none in every draw.
All inputs are finite; a program needn't handle non-finite values.
Results may differ from a plain program's by a relative error of at most 0.0019.
The roundings to bfloat16 on the way count: a program that leaves them out, or rounds other values in their place, can miss the bound.
Values may be sent and summed in bfloat16 or wider, within the bound.
A program may use at most 384 MiB of HBM per device.

v0:
```python
import jax
import jax.numpy as jnp
from jax import lax
from jax.sharding import PartitionSpec as P

GROUPS = 32
H = 64
W = 64
NETS = 3


EPSILON = 1e-05


def extended(x, sides, width):
    for axis, dim in sides:
        size, length = (lax.axis_size(axis), x.shape[dim])
        up = [(i, (i + 1) % size) for i in range(size - 1)]
        down = [(j, i) for i, j in up]
        last = lax.slice_in_dim(x, length - width, length, axis=dim)
        initial = lax.slice_in_dim(x, 0, width, axis=dim)
        before = lax.ppermute(last, axis, up)
        after = lax.ppermute(initial, axis, down)
        x = jnp.concatenate([before, x, after], axis=dim)
    return x


def group_sums(value, groups):
    batch, height, across, chans = value.shape
    return jnp.sum(value.reshape(batch, height, across, groups, chans // groups), axis=(1, 2, 4))


def spread_groups(stat, chans):
    return jnp.repeat(stat, chans // stat.shape[1], axis=1)[:, None, None, :]


def normalize(value, groups):
    chans = value.shape[3]
    first_sum = group_sums(value, groups)
    second_sum = group_sums(value * value, groups)
    first_sum, second_sum = lax.psum((first_sum, second_sum), "fsdp")
    count = H * W * (chans // groups)
    mean_value = first_sum / count
    variance = second_sum / count - mean_value * mean_value
    inverse = lax.rsqrt(variance + EPSILON)
    return ((value - spread_groups(mean_value, chans)) * spread_groups(inverse, chans), inverse)


def norm_totals(first_part, second_part):
    return lax.psum((first_part, second_part), "fsdp")


def norm_finish(scaled_grad, normed, inverse, first_total, second_total, groups):
    chans = normed.shape[3]
    count = H * W * (chans // groups)
    centered = scaled_grad - spread_groups(first_total / count, chans)
    return spread_groups(inverse, chans) * (
        centered - normed * spread_groups(second_total / count, chans)
    )


def pad_rows(activation):
    padded = extended(activation, (("fsdp", 1),), 1)
    return jnp.pad(padded, ((0, 0), (0, 0), (1, 1), (0, 0)))


def pad_grads(gradient):
    padded = extended(gradient, (("fsdp", 1),), 1)
    return jnp.pad(padded, ((0, 0), (0, 0), (1, 1), (0, 0)))


def conv_apply(padded, kernel):
    height = padded.shape[1] - 2
    across = padded.shape[2] - 2
    total = jnp.zeros((padded.shape[0], height, across, kernel.shape[3]), jnp.float32)
    for row_tap in range(3):
        for col_tap in range(3):
            window = padded[:, row_tap : row_tap + height, col_tap : col_tap + across, :]
            total = total + jnp.einsum(
                "bhwc,cd->bhwd",
                window,
                kernel[row_tap, col_tap],
                preferred_element_type=jnp.float32,
            )
    return total


def conv_back(padded, kernel):
    height = padded.shape[1] - 2
    across = padded.shape[2] - 2
    total = jnp.zeros((padded.shape[0], height, across, kernel.shape[2]), jnp.float32)
    for row_tap in range(3):
        for col_tap in range(3):
            window = padded[
                :, 2 - row_tap : 2 - row_tap + height, 2 - col_tap : 2 - col_tap + across, :
            ]
            total = total + jnp.einsum(
                "bhwd,cd->bhwc",
                window,
                kernel[row_tap, col_tap],
                preferred_element_type=jnp.float32,
            )
    return total


def kernel_grad(padded, gradient):
    height = gradient.shape[1]
    across = gradient.shape[2]
    tap_rows = []
    for row_tap in range(3):
        tap_cols = []
        for col_tap in range(3):
            window = padded[:, row_tap : row_tap + height, col_tap : col_tap + across, :]
            tap_cols.append(
                jnp.einsum("bhwc,bhwd->cd", window, gradient, preferred_element_type=jnp.float32)
            )
        tap_rows.append(jnp.stack(tap_cols))
    return jnp.stack(tap_rows)


def silu_slope(value):
    sigmoid_value = jax.nn.sigmoid(value)
    return sigmoid_value * (1.0 + value * (1.0 - sigmoid_value))


def on_device(
    block_input, embedding, out_cotangent, conv_weights, affine_weight, gains, biases, counts
):
    slot_count = block_input.shape[1]
    channels = block_input.shape[4]
    shard_count = lax.axis_size("fsdp")
    shard_index = lax.axis_index("fsdp")
    chan_piece = channels // shard_count
    keep_mask = (jnp.arange(slot_count) < counts[0]).astype(jnp.float32)
    keep_four = keep_mask[:, None, None, None]
    outputs = []
    in_grads = []
    conv_list = []
    affine_list = []
    gain_list = []
    bias_list = []
    for network in range(NETS):
        image_float = block_input[network].astype(jnp.float32)
        kernels, affine, gain_row, bias_row = (
            lax.all_gather(conv_weights[network], "fsdp", axis=3, tiled=True),
            lax.all_gather(affine_weight[network], "fsdp", axis=0, tiled=True),
            lax.all_gather(gains[network], "fsdp", axis=1, tiled=True),
            lax.all_gather(biases[network], "fsdp", axis=1, tiled=True),
        )
        gain_float = gain_row.astype(jnp.float32)
        bias_float = bias_row.astype(jnp.float32)
        normed_zero, inverse_zero = normalize(image_float, GROUPS)
        zeroth = normed_zero * gain_float[0] + bias_float[0]
        first_act = jax.nn.silu(zeroth).astype(jnp.bfloat16)
        padded_zero = pad_rows(first_act)
        hidden = conv_apply(padded_zero, kernels[0]) + bias_float[1]
        normed_one, inverse_one = normalize(hidden, GROUPS)
        first_mod = normed_one * gain_float[1] + bias_float[2]
        embed_rows = embedding[network]
        projection = jnp.dot(embed_rows, affine, preferred_element_type=jnp.float32)
        projection = projection + jnp.concatenate([bias_float[4], bias_float[5]])
        scale_part = projection[:, :channels][:, None, None, :]
        shift_part = projection[:, channels:][:, None, None, :]
        pre_act = shift_part + first_mod * (scale_part + 1.0)
        second_act = jax.nn.silu(pre_act).astype(jnp.bfloat16)
        padded_one = pad_rows(second_act)
        branch = conv_apply(padded_one, kernels[1]) + bias_float[3]
        outputs.append(((branch + image_float) * keep_four).astype(jnp.bfloat16))
        back_kernels, back_gain_row = (
            lax.all_gather(conv_weights[network], "fsdp", axis=3, tiled=True),
            lax.all_gather(gains[network], "fsdp", axis=1, tiled=True),
        )
        back_gain = back_gain_row.astype(jnp.float32)
        grad_out = out_cotangent[network] * keep_four.astype(jnp.bfloat16)
        grad_float = grad_out.astype(jnp.float32)
        act_grad = conv_back(pad_grads(grad_out), back_kernels[1])
        pre_grad = act_grad * silu_slope(pre_act)
        mod_grad = pre_grad * (scale_part + 1.0)
        scaled_one = mod_grad * back_gain[1]
        first_part = group_sums(scaled_one, GROUPS)
        second_part = group_sums(scaled_one * normed_one, GROUPS)
        trainable = network != 1
        if trainable:
            scale_sum = jnp.sum(pre_grad * first_mod, axis=(1, 2))
            shift_sum = jnp.sum(pre_grad, axis=(1, 2))
            first_total, second_total, scale_sum, shift_sum = lax.psum(
                (first_part, second_part, scale_sum, shift_sum), "fsdp"
            )
        else:
            first_total, second_total = norm_totals(first_part, second_part)
        hidden_grad = norm_finish(
            scaled_one, normed_one, inverse_one, first_total, second_total, GROUPS
        )
        hidden_low = hidden_grad.astype(jnp.bfloat16)
        zero_grad = conv_back(pad_grads(hidden_low), back_kernels[0]) * silu_slope(zeroth)
        scaled_zero = zero_grad * back_gain[0]
        first_total, second_total = norm_totals(
            group_sums(scaled_zero, GROUPS), group_sums(scaled_zero * normed_zero, GROUPS)
        )
        input_part = norm_finish(
            scaled_zero, normed_zero, inverse_zero, first_total, second_total, GROUPS
        )
        in_grads.append((grad_float + input_part).astype(jnp.bfloat16))
        if trainable:
            kernel_total = jnp.stack(
                [kernel_grad(padded_zero, hidden_low), kernel_grad(padded_one, grad_out)]
            )
            gain_total = jnp.stack(
                [
                    jnp.sum(zero_grad * normed_zero, axis=(0, 1, 2)),
                    jnp.sum(mod_grad * normed_one, axis=(0, 1, 2)),
                ]
            )
            pixel_bias = jnp.stack(
                [
                    jnp.sum(zero_grad, axis=(0, 1, 2)),
                    jnp.sum(hidden_grad, axis=(0, 1, 2)),
                    jnp.sum(mod_grad, axis=(0, 1, 2)),
                    jnp.sum(grad_float, axis=(0, 1, 2)),
                ]
            )
            mod_total = jnp.concatenate([scale_sum, shift_sum], axis=1)
            mod_low = mod_total.astype(jnp.bfloat16)
            embed_piece_rows = embed_rows.shape[1] // shard_count
            embed_piece = lax.dynamic_slice_in_dim(
                embed_rows, shard_index * embed_piece_rows, embed_piece_rows, 1
            )
            affine_piece = jnp.einsum(
                "be,bd->ed", embed_piece, mod_low, preferred_element_type=jnp.float32
            )
            mod_bias = jnp.sum(mod_total, axis=0).reshape(2, channels)
            mod_piece = lax.dynamic_slice_in_dim(mod_bias, shard_index * chan_piece, chan_piece, 1)
            kernel_piece, gain_piece, bias_piece = (
                lax.psum_scatter(kernel_total, "fsdp", scatter_dimension=3, tiled=True),
                lax.psum_scatter(gain_total, "fsdp", scatter_dimension=1, tiled=True),
                lax.psum_scatter(pixel_bias, "fsdp", scatter_dimension=1, tiled=True),
            )
            kernel_piece, gain_piece, bias_six, affine_sum = lax.psum(
                (
                    kernel_piece,
                    gain_piece,
                    jnp.concatenate([bias_piece, mod_piece], axis=0),
                    affine_piece,
                ),
                "dp",
            )
            conv_list.append(kernel_piece)
            affine_list.append(affine_sum)
            gain_list.append(gain_piece)
            bias_list.append(bias_six)
    return (
        jnp.stack(outputs),
        jnp.stack(in_grads),
        jnp.stack(conv_list),
        jnp.stack(affine_list),
        jnp.stack(gain_list),
        jnp.stack(bias_list),
    )


def solution(mesh):
    placed = (
        P(None, "dp", "fsdp", None, None),
        P(None, "dp", None),
        P(None, "dp", "fsdp", None, None),
        P(None, None, None, None, "fsdp", None),
        P(None, "fsdp", None),
        P(None, None, "fsdp"),
        P(None, None, "fsdp"),
        P("dp"),
    )
    return jax.shard_map(
        on_device,
        mesh=mesh,
        in_specs=placed,
        out_specs=(
            P(None, "dp", "fsdp", None, None),
            P(None, "dp", "fsdp", None, None),
            P(None, None, None, None, "fsdp", None),
            P(None, "fsdp", None),
            P(None, None, "fsdp"),
            P(None, None, "fsdp"),
        ),
        check_vma=False,
    )
```

profile of v0, /device:TPU:0, one launch (start us, length us, event | category | flops | bytes accessed | tf_op | source)
XLA Modules:
  0.0 1004.5 jit_solution(2512885163900047442)
XLA Ops:
  11.5 5.7 all-gather.9
  21.7 5.8 all-gather.10
  31.3 5.8 all-gather.1
  41.7 4.9 all-gather.2
  55.4 5.2 all-reduce.17
  61.5 5.8 all-gather.5
  71.8 5.8 all-gather.6
  81.7 6.1 fusion.66
  89.2 4.5 collective-permute-start.8
  95.0 4.5 collective-permute-start.4
  101.9 4.7 convert_reduce_fusion.4
  110.0 17.0 %all-gather.8 = bf16[1,768,384]{2,1,0:T(8,128)(2,1)S(1)} all-gather(bf16[1,384,384]{2,1,0:T(8,128)(2,1)S(1)} %get-tuple-element.181), channel_id=10, replica_groups=mesh['dp'=16,'fsdp'=2] {'fsdp'}, dimensions={1}, use_global_device_ids=true | all-gather | bytes 884736 | tf_op jit(solution)/shard_map/all_gather | solution.py:146
  128.5 17.0 %all-gather = bf16[1,768,384]{2,1,0:T(8,128)(2,1)S(1)} all-gather(bf16[1,384,384]{2,1,0:T(8,128)(2,1)S(1)} %get-tuple-element.180), channel_id=2, replica_groups=mesh['dp'=16,'fsdp'=2] {'fsdp'}, dimensions={1}, use_global_device_ids=true | all-gather | bytes 884736 | tf_op jit(solution)/shard_map/all_gather | solution.py:146
  146.5 7.4 all-gather.4
  163.0 4.5 collective-permute-start.20
  172.4 4.5 collective-permute-start.12
  180.6 4.7 collective-permute-start.16
  200.3 5.1 fusion.176
  229.5 5.2 fusion.179
  242.3 5.3 fusion.182
  312.2 12.0 %fusion.607 = (f32[2,192]{1,0:T(2,128)}, f32[2,192]{1,0:T(2,128)}, f32[2,32,64,192]{3,2,1,0:T(8,128)}) fusion(f32[192]{0:T(256)S(1)} %get-tuple-element.86, bf16[3,3,192,192]{3,2,1,0:T(8,128)(2,1)} %copy-done.72, bf16[2,34,66,192]{3,2,1,0:T(8,128)(2,1)S(1)} %select_maximum_fusion.14, f32[2,32,64,192]{3,2,1,0:T(8,128)} %fusion.439, ...), kind=kOutput, calls=%fused_computation.778 | convolution fusion | flops 311426304 | bytes 38899712 | tf_op jit(solution)/shard_map/bhwc,cd->bhwd/dot_general | solution.py:79
  335.2 13.2 %fusion.606 = (f32[2,192]{1,0:T(2,128)}, f32[2,192]{1,0:T(2,128)}, f32[2,32,64,192]{3,2,1,0:T(8,128)}) fusion(f32[192]{0:T(256)S(1)} %copy-done.173, bf16[3,3,192,192]{3,2,1,0:T(8,128)(2,1)} %copy-done.70, bf16[2,34,66,192]{3,2,1,0:T(8,128)(2,1)S(1)} %copy-done.27, f32[2,32,64,192]{3,2,1,0:T(8,128)} %fusion.115, f32[2,32,64,192]{3,2,1,0:T(8,128)S(1)} %copy-done.58, ...), kind=kOutput, calls=%fused_computation.777 | convolution fusion | flops 311426304 | bytes 38899712 | tf_op jit(solution)/shard_map/bhwc,cd->bhwd/dot_general | solution.py:79
  351.3 4.5 fusion.447
  359.5 13.2 %fusion.605 = (f32[2,192]{1,0:T(2,128)}, f32[2,192]{1,0:T(2,128)}, f32[2,32,64,192]{3,2,1,0:T(8,128)}) fusion(f32[192]{0:T(256)S(1)} %copy-done.172, bf16[3,3,192,192]{3,2,1,0:T(8,128)(2,1)} %copy-done.75, bf16[2,34,66,192]{3,2,1,0:T(8,128)(2,1)S(1)} %copy-done.1, f32[2,32,64,192]{3,2,1,0:T(8,128)} %fusion.447, f32[2,32,64,192]{3,2,1,0:T(8,128)S(1)} %copy-done.57, ...), kind=kOutput, calls=%fused_computation.776 | convolution fusion | flops 311426304 | bytes 38899712 | tf_op jit(solution)/shard_map/bhwc,cd->bhwd/dot_general | solution.py:79
  375.6 6.1 all-reduce.16
  392.8 16.0 %multiply_reduce_fusion.11 = (f32[2,192]{1,0:T(2,128)}, f32[2,192]{1,0:T(2,128)}, f32[2,32,64,192]{3,2,1,0:T(8,128)}) fusion(f32[2,192]{1,0:T(2,128)S(1)} %copy-done.144, f32[192]{0:T(256)S(1)} %copy-done.160, f32[2,192]{1,0:T(2,128)S(1)} %copy-done.139, f32[2,32,64,192]{3,2,1,0:T(8,128)} %get-tuple-element.209, f32[2,192]{1,0:T(2,128)S(1)} %copy-done.140, ...), kind=kOutput, calls=%fused_computation.160 | convolution fusion | flops 323222784 | bytes 43103232 | tf_op jit(solution)/shard_map/bhwd,cd->bhwc/dot_general | solution.py:97
  422.4 16.7 %multiply_reduce_fusion.13 = (f32[2,192]{1,0:T(2,128)}, f32[2,192]{1,0:T(2,128)}, f32[2,32,64,192]{3,2,1,0:T(8,128)}) fusion(f32[2,192]{1,0:T(2,128)S(1)} %copy-done.142, f32[192]{0:T(256)S(1)} %copy-done.158, f32[2,192]{1,0:T(2,128)S(1)} %copy-done.137, f32[2,32,64,192]{3,2,1,0:T(8,128)} %get-tuple-element.211, f32[2,192]{1,0:T(2,128)S(1)} %copy-done.138, ...), kind=kOutput, calls=%fused_computation.162 | convolution fusion | flops 323222784 | bytes 33666048 | tf_op jit(solution)/shard_map/bhwd,cd->bhwc/dot_general | solution.py:97
  453.5 16.0 %fusion.604 = (f32[2,192]{1,0:T(2,128)}, f32[2,192]{1,0:T(2,128)}, f32[2,32,64,192]{3,2,1,0:T(8,128)}) fusion(f32[2,192]{1,0:T(2,128)S(1)} %copy-done.145, f32[2,32,64,192]{3,2,1,0:T(8,128)} %get-tuple-element.210, f32[2,192]{1,0:T(2,128)S(1)} %copy-done.146, f32[2,192]{1,0:T(2,128)S(1)} %copy-done.148, f32[192]{0:T(256)S(1)} %copy-done.161, ...), kind=kOutput, calls=%fused_computation.775 | convolution fusion | flops 323222784 | bytes 43103232 | tf_op jit(solution)/shard_map/bhwd,cd->bhwc/dot_general | solution.py:97
  472.3 5.8 all-reduce.15
  480.3 8.1 fusion.542
  495.5 5.7 multiply_convert_fusion
  508.3 7.4 fusion.540
  544.8 4.5 collective-permute-start.10
  550.6 5.1 collective-permute-start.22
  561.8 4.5 collective-permute-start.18
  583.8 4.5 collective-permute-start.14
  617.7 4.5 collective-permute-start.2
  648.5 15.0 %fusion.24 = f32[2,32,64,192]{3,2,1,0:T(8,128)} fusion(f32[2,32,64,192]{3,2,1,0:T(8,128)} %fusion.171, f32[2,32,64,192]{3,2,1,0:T(8,128)} %fusion.189, f32[2,32,64,192]{3,2,1,0:T(8,128)} %fusion.191, f32[2,32,64,192]{3,2,1,0:T(8,128)} %fusion.548, f32[2,32,64,192]{3,2,1,0:T(8,128)} %fusion.193, f32[2,32,64,192]{3,2,1,0:T(8,128)} %fusion.195, ...), kind=kOutput, calls=%fused_computation.44 | convolution fusion | flops 318504960 | bytes 40998912 | tf_op jit(solution)/shard_map/bhwd,cd->bhwc/dot_general | solution.py:97
  669.1 15.3 %fusion.46 = f32[2,32,64,192]{3,2,1,0:T(8,128)} fusion(f32[2,32,64,192]{3,2,1,0:T(8,128)} %fusion.155, f32[2,32,64,192]{3,2,1,0:T(8,128)} %fusion.213, f32[2,32,64,192]{3,2,1,0:T(8,128)} %fusion.215, f32[2,32,64,192]{3,2,1,0:T(8,128)} %fusion.546, f32[2,32,64,192]{3,2,1,0:T(8,128)} %fusion.217, f32[2,32,64,192]{3,2,1,0:T(8,128)} %fusion.219, ...), kind=kOutput, calls=%fused_computation.66 | convolution fusion | flops 319291392 | bytes 32086016 | tf_op jit(solution)/shard_map/bhwd,cd->bhwc/dot_general | solution.py:97
  691.7 21.9 %fusion.73 = (f32[192]{0:T(256)}, f32[2,192]{1,0:T(2,128)S(1)}, f32[2,192]{1,0:T(2,128)S(1)}, f32[192]{0:T(256)}, f32[2,192]{1,0:T(2,128)S(1)}, /*index=5*/f32[2...) fusion(f32[2,192]{1,0:T(2,128)S(1)} %copy-done.154, ...), kind=kOutput, calls=%fused_computation.93 | convolution fusion | flops 336589824 | bytes 53599488 | tf_op jit(solution)/shard_map/bhwd,cd->bhwc/dot_general | solution.py:97
  718.6 7.5 all-reduce.14
  789.9 5.2 fusion.184
  812.5 14.0 %fusion.312 = bf16[1,2,32,64,192]{4,3,2,1,0:T(8,128)(2,1)} fusion(f32[2]{0:T(128)S(1)} %copy-done.152, f32[192]{0:T(256)S(1)} %copy-done.170, f32[2,32,64,192]{3,2,1,0:T(8,128)} %fusion.435, f32[2,32,64,192]{3,2,1,0:T(8,128)} %fusion.321, f32[2,32,64,192]{3,2,1,0:T(8,128)} %fusion.325, f32[2,32,64,192]{3,2,1,0:T(8,128)} %fusion.549, ...), kind=kOutput, calls=%fused_computation.400 | convolution fusion | flops 312213504 | bytes 39421440 | tf_op jit(solution)/shard_map/bhwc,cd->bhwd/dot_general | solution.py:79
  834.0 14.0 %fusion.432 = bf16[1,2,32,64,192]{4,3,2,1,0:T(8,128)(2,1)} fusion(f32[2]{0:T(128)S(1)} %copy-done.152, f32[192]{0:T(256)S(1)} %copy-done.171, bf16[2,34,66,192]{3,2,1,0:T(8,128)(2,1)S(1)} %copy-done.29, f32[2,32,64,192]{3,2,1,0:T(8,128)} %fusion.123, f32[2,32,64,192]{3,2,1,0:T(8,128)} %fusion.263, f32[2,32,64,192]{3,2,1,0:T(8,128)} %fusion.265, ...), kind=kOutput, calls=%fused_computation.504 | convolution fusion | flops 312213504 | bytes 39421440 | tf_op jit(solution)/shard_map/bhwc,cd->bhwd/dot_general | solution.py:79
  853.4 12.5 %fusion.311 = bf16[1,2,32,64,192]{4,3,2,1,0:T(8,128)(2,1)S(1)} fusion(f32[2]{0:T(128)S(1)} %copy-done.152, f32[192]{0:T(256)S(1)} %copy-done.169, f32[2,32,64,192]{3,2,1,0:T(8,128)} %fusion.443, f32[2,32,64,192]{3,2,1,0:T(8,128)} %fusion.373, f32[2,32,64,192]{3,2,1,0:T(8,128)} %fusion.377, f32[2,32,64,192]{3,2,1,0:T(8,128)} %fusion.545, ...), kind=kOutput, calls=%fused_computation.399 | convolution fusion | flops 312213504 | bytes 30508544 | tf_op jit(solution)/shard_map/bhwc,cd->bhwd/dot_general | solution.py:79
  873.0 6.9 fusion.186
  887.3 59.0 %all-reduce.12 = (f32[1,2,96]{2,1,0:T(2,128)S(1)}, f32[1,2,96]{2,1,0:T(2,128)S(1)}, f32[1,6,96]{2,1,0:T(8,128)S(1)}, f32[1,6,96]{2,1,0:T(8,128)S(1)}) all-reduce(f32[1,2,96]{2,1,0:T(2,128)S(1)} %bitcast.1051, f32[1,2,96]{2,1,0:T(2,128)S(1)} %bitcast.1052, ...), channel_id=1, replica_groups=mesh['dp'=16,'fsdp'=2] {'dp'}, use_global_device_ids=true, to_apply=%region_93.94 | all-reduce | flops 1536 | bytes 12288 | tf_op jit(solution)/shard_map/psum | solution.py:238
  947.4 44.7 %all-reduce.20.cloned.1.call-done = (f32[1,2,3,3,96,192]{5,4,3,2,1,0:T(8,128)}, f32[1,2,3,3,96,192]{5,4,3,2,1,0:T(8,128)}, f32[1,384,384]{2,1,0:T(8,128)}, f32[1,384,384]{2,1,0:T(8,128)}) async-done(((f32[1,2,3,3,96,192]{5,4,3,2,1,0:T(8,128)}, f32[1,2,3,3,96,192]{5,4,3,2,1,0:T(8,128)}, f32[1,384,384]{2,1,0:T(8,128)}, f32[1,384,384]{2,1,0:T(8,128)}), (f32[1,2,3,3,96,192]{5,4,3,2,1,0:T(8,128)}, ...) | async-done | bytes 3833872 | tf_op jit(solution)/shard_map/psum | solution.py:238
  (829 shorter events, 493.0 us)
Async XLA Ops:
  7.2 185.2 %all-gather.20.cloned.1.call-start = ((), (), s32[]{:S(2)}) async-start(), calls=%async_computation.10 | async-start | bytes 2654208 | tf_op jit(solution)/shard_map/all_gather | solution.py:145
  10.5 202.9 %all-gather.18.cloned.1.call-start = ((), (), s32[]{:S(2)}) async-start(), calls=%async_computation.9 | async-start | bytes 2654208 | tf_op jit(solution)/shard_map/all_gather | solution.py:145
  11.3 223.4 %all-gather.16.cloned.1.call-start = ((), (), s32[]{:S(2)}) async-start(), calls=%async_computation.8 | async-start | bytes 2654208 | tf_op jit(solution)/shard_map/all_gather | solution.py:145
  21.6 178.7 %copy-start.163 = (f32[192]{0:T(256)}, f32[192]{0:T(256)S(1)}, u32[]{:S(2)}) copy-start(f32[192]{0:T(256)S(1)} %get-tuple-element.88) | copy-start | bytes 2308
  31.2 169.1 %copy-start.150 = (f32[192]{0:T(256)}, f32[192]{0:T(256)S(1)}, u32[]{:S(2)}) copy-start(f32[192]{0:T(256)S(1)} %get-tuple-element.92) | copy-start | bytes 2308
  50.2 192.1 %copy-start.174 = (f32[192]{0:T(256)}, f32[192]{0:T(256)S(1)}, u32[]{:S(2)}) copy-start(f32[192]{0:T(256)S(1)} %get-tuple-element.76) | copy-start | bytes 2308
  60.8 181.5 %copy-start.153 = (f32[2,192]{1,0:T(2,128)}, f32[2,192]{1,0:T(2,128)S(1)}, u32[]{:S(2)}) copy-start(f32[2,192]{1,0:T(2,128)S(1)} %mul.551) | copy-start | bytes 4612
  61.0 181.4 %copy-start.155 = (f32[2,192]{1,0:T(2,128)}, f32[2,192]{1,0:T(2,128)S(1)}, u32[]{:S(2)}) copy-start(f32[2,192]{1,0:T(2,128)S(1)} %sub.189) | copy-start | bytes 4612
  61.2 139.1 %copy-start.127 = (f32[2,192]{1,0:T(2,128)}, f32[2,192]{1,0:T(2,128)S(1)}, u32[]{:S(2)}) copy-start(f32[2,192]{1,0:T(2,128)S(1)} %mul.604) | copy-start | bytes 4612
  61.4 138.9 %copy-start.129 = (f32[2,192]{1,0:T(2,128)}, f32[2,192]{1,0:T(2,128)S(1)}, u32[]{:S(2)}) copy-start(f32[2,192]{1,0:T(2,128)S(1)} %sub.209) | copy-start | bytes 4612
  71.7 157.7 %copy-start.165 = (f32[192]{0:T(256)}, f32[192]{0:T(256)S(1)}, u32[]{:S(2)}) copy-start(f32[192]{0:T(256)S(1)} %get-tuple-element.82) | copy-start | bytes 2308
  81.3 148.2 %copy-start.167 = (f32[192]{0:T(256)}, f32[192]{0:T(256)S(1)}, u32[]{:S(2)}) copy-start(f32[192]{0:T(256)S(1)} %get-tuple-element.79) | copy-start | bytes 2308
  81.5 148.0 %copy-start.131 = (f32[2,192]{1,0:T(2,128)}, f32[2,192]{1,0:T(2,128)S(1)}, u32[]{:S(2)}) copy-start(f32[2,192]{1,0:T(2,128)S(1)} %mul.578) | copy-start | bytes 4612
  81.7 147.8 %copy-start.133 = (f32[2,192]{1,0:T(2,128)}, f32[2,192]{1,0:T(2,128)S(1)}, u32[]{:S(2)}) copy-start(f32[2,192]{1,0:T(2,128)S(1)} %sub.199) | copy-start | bytes 4612
  87.9 68.2 %collective-permute-start.9 = (bf16[2,1,64,192]{3,2,1,0:T(8,128)(2,1)S(1)}, bf16[2,1,64,192]{3,2,1,0:T(8,128)(2,1)S(1)}, u32[]{:S(2)}, u32[]{:S(2)}) collective-permute-start(bf16[2,1,64,192]{3,2,1,0:T(8,128)(2,1)S(1)} %get-tuple-element.173), channel_id=1, source_target_pairs={{1,0},{3,2},{5,4},{7,6},{9,8},{11,10},{13,12},{15,14},{17,16},{19,... | collective-permute-start | bytes 147464 | tf_op jit(solution)/shard_map/ppermute | solution.py:23
  89.2 70.1 %collective-permute-start.8 = (bf16[2,1,64,192]{3,2,1,0:T(8,128)(2,1)S(1)}, bf16[2,1,64,192]{3,2,1,0:T(8,128)(2,1)S(1)}, u32[]{:S(2)}, u32[]{:S(2)}) collective-permute-start(bf16[2,1,64,192]{3,2,1,0:T(8,128)(2,1)S(1)} %get-tuple-element.172), channel_id=1, source_target_pairs={{0,1},{2,3},{4,5},{6,7},{8,9},{10,11},{12,13},{14,15},{16,17},{18,... | collective-permute-start | bytes 147464 | tf_op jit(solution)/shard_map/ppermute | solution.py:22
  93.7 69.3 %collective-permute-start.5 = (bf16[2,1,64,192]{3,2,1,0:T(8,128)(2,1)S(1)}, bf16[2,1,64,192]{3,2,1,0:T(8,128)(2,1)S(1)}, u32[]{:S(2)}, u32[]{:S(2)}) collective-permute-start(bf16[2,1,64,192]{3,2,1,0:T(8,128)(2,1)S(1)} %get-tuple-element.171), channel_id=1, source_target_pairs={{1,0},{3,2},{5,4},{7,6},{9,8},{11,10},{13,12},{15,14},{17,16},{19,... | collective-permute-start | bytes 147464 | tf_op jit(solution)/shard_map/ppermute | solution.py:23
  95.0 72.5 %collective-permute-start.4 = (bf16[2,1,64,192]{3,2,1,0:T(8,128)(2,1)S(1)}, bf16[2,1,64,192]{3,2,1,0:T(8,128)(2,1)S(1)}, u32[]{:S(2)}, u32[]{:S(2)}) collective-permute-start(bf16[2,1,64,192]{3,2,1,0:T(8,128)(2,1)S(1)} %get-tuple-element.170), channel_id=1, source_target_pairs={{0,1},{2,3},{4,5},{6,7},{8,9},{10,11},{12,13},{14,15},{16,17},{18,... | collective-permute-start | bytes 147464 | tf_op jit(solution)/shard_map/ppermute | solution.py:22
  99.6 72.7 %collective-permute-start.1 = (bf16[2,1,64,192]{3,2,1,0:T(8,128)(2,1)S(1)}, bf16[2,1,64,192]{3,2,1,0:T(8,128)(2,1)S(1)}, u32[]{:S(2)}, u32[]{:S(2)}) collective-permute-start(bf16[2,1,64,192]{3,2,1,0:T(8,128)(2,1)S(1)} %get-tuple-element.169), channel_id=1, source_target_pairs={{1,0},{3,2},{5,4},{7,6},{9,8},{11,10},{13,12},{15,14},{17,16},{19,... | collective-permute-start | bytes 147464 | tf_op jit(solution)/shard_map/ppermute | solution.py:23
  101.0 771.2 %reduce-scatter.17.cloned.1.call-start = ((), (), s32[]{:S(2)}) async-start(), calls=%async_computation.7 | async-start | bytes 5308416 | tf_op jit(solution)/shard_map/reduce_scatter | solution.py:234
  101.9 191.9 %copy-start.135 = (bf16[2]{0:T(256)(128)(2,1)}, bf16[2]{0:T(256)(128)(2,1)S(1)}, u32[]{:S(2)}) copy-start(bf16[2]{0:T(256)(128)(2,1)S(1)} %fusion.601) | copy-start | bytes 16
  156.0 20.9 %collective-permute-start = (bf16[2,1,64,192]{3,2,1,0:T(8,128)(2,1)S(1)}, bf16[2,1,64,192]{3,2,1,0:T(8,128)(2,1)S(1)}, u32[]{:S(2)}, u32[]{:S(2)}) collective-permute-start(bf16[2,1,64,192]{3,2,1,0:T(8,128)(2,1)S(1)} %get-tuple-element.168), channel_id=1, source_target_pairs={{0,1},{2,3},{4,5},{6,7},{8,9},{10,11},{12,13},{14,15},{16,17},{18,... | collective-permute-start | bytes 147464 | tf_op jit(solution)/shard_map/ppermute | solution.py:22
  159.2 21.3 %collective-permute-start.21 = (bf16[2,1,64,192]{3,2,1,0:T(8,128)(2,1)S(1)}, bf16[2,1,64,192]{3,2,1,0:T(8,128)(2,1)S(1)}, u32[]{:S(2)}, u32[]{:S(2)}) collective-permute-start(bf16[2,1,64,192]{3,2,1,0:T(8,128)(2,1)S(1)} %get-tuple-element.160), channel_id=1, source_target_pairs={{1,0},{3,2},{5,4},{7,6},{9,8},{11,10},{13,12},{15,14},{17,16},{19,... | collective-permute-start | bytes 147464 | tf_op jit(solution)/shard_map/ppermute | solution.py:23
  163.0 22.3 %collective-permute-start.20 = (bf16[2,1,64,192]{3,2,1,0:T(8,128)(2,1)S(1)}, bf16[2,1,64,192]{3,2,1,0:T(8,128)(2,1)S(1)}, u32[]{:S(2)}, u32[]{:S(2)}) collective-permute-start(bf16[2,1,64,192]{3,2,1,0:T(8,128)(2,1)S(1)} %get-tuple-element.161), channel_id=1, source_target_pairs={{0,1},{2,3},{4,5},{6,7},{8,9},{10,11},{12,13},{14,15},{16,17},{18,... | collective-permute-start | bytes 147464 | tf_op jit(solution)/shard_map/ppermute | solution.py:22
  167.6 19.9 %collective-permute-start.13 = (bf16[2,1,64,192]{3,2,1,0:T(8,128)(2,1)S(1)}, bf16[2,1,64,192]{3,2,1,0:T(8,128)(2,1)S(1)}, u32[]{:S(2)}, u32[]{:S(2)}) collective-permute-start(bf16[2,1,64,192]{3,2,1,0:T(8,128)(2,1)S(1)} %get-tuple-element.158), channel_id=1, source_target_pairs={{1,0},{3,2},{5,4},{7,6},{9,8},{11,10},{13,12},{15,14},{17,16},{19,... | collective-permute-start | bytes 147464 | tf_op jit(solution)/shard_map/ppermute | solution.py:23
  172.4 15.2 %collective-permute-start.12 = (bf16[2,1,64,192]{3,2,1,0:T(8,128)(2,1)S(1)}, bf16[2,1,64,192]{3,2,1,0:T(8,128)(2,1)S(1)}, u32[]{:S(2)}, u32[]{:S(2)}) collective-permute-start(bf16[2,1,64,192]{3,2,1,0:T(8,128)(2,1)S(1)} %get-tuple-element.159), channel_id=1, source_target_pairs={{0,1},{2,3},{4,5},{6,7},{8,9},{10,11},{12,13},{14,15},{16,17},{18,... | collective-permute-start | bytes 147464 | tf_op jit(solution)/shard_map/ppermute | solution.py:22
  177.0 12.8 %collective-permute-start.17 = (bf16[2,1,64,192]{3,2,1,0:T(8,128)(2,1)S(1)}, bf16[2,1,64,192]{3,2,1,0:T(8,128)(2,1)S(1)}, u32[]{:S(2)}, u32[]{:S(2)}) collective-permute-start(bf16[2,1,64,192]{3,2,1,0:T(8,128)(2,1)S(1)} %copy-done.126), channel_id=1, source_target_pairs={{1,0},{3,2},{5,4},{7,6},{9,8},{11,10},{13,12},{15,14},{17,16},{19,... | collective-permute-start | bytes 147464 | tf_op jit(solution)/shard_map/ppermute | solution.py:23
  180.6 9.2 collective-permute-start.16
  236.4 279.3 %copy-start.65 = (bf16[3,3,192,192]{3,2,1,0:T(8,128)(2,1)}, bf16[3,3,192,192]{3,2,1,0:T(8,128)(2,1)S(1)}, u32[]{:S(2)}) copy-start(bf16[3,3,192,192]{3,2,1,0:T(8,128)(2,1)S(1)} %get-tuple-element.174) | copy-start | bytes 1990660
  515.7 115.1 %copy-start.37 = (bf16[2,32,64,192]{3,2,1,0:T(8,128)(2,1)}, bf16[2,32,64,192]{3,2,1,0:T(8,128)(2,1)S(1)}, u32[]{:S(2)}) copy-start(bf16[2,32,64,192]{3,2,1,0:T(8,128)(2,1)S(1)} %get-tuple-element.143) | copy-start | bytes 4718596
  543.4 74.2 %collective-permute-start.11 = (bf16[2,1,64,192]{3,2,1,0:T(8,128)(2,1)S(1)}, bf16[2,1,64,192]{3,2,1,0:T(8,128)(2,1)S(1)}, u32[]{:S(2)}, u32[]{:S(2)}) collective-permute-start(bf16[2,1,64,192]{3,2,1,0:T(8,128)(2,1)S(1)} %copy-done.124), channel_id=1, source_target_pairs={{1,0},{3,2},{5,4},{7,6},{9,8},{11,10},{13,12},{15,14},{17,16},{19,... | collective-permute-start | bytes 147464 | tf_op jit(solution)/shard_map/ppermute | solution.py:23
  544.8 77.5 %collective-permute-start.10 = (bf16[2,1,64,192]{3,2,1,0:T(8,128)(2,1)S(1)}, bf16[2,1,64,192]{3,2,1,0:T(8,128)(2,1)S(1)}, u32[]{:S(2)}, u32[]{:S(2)}) collective-permute-start(bf16[2,1,64,192]{3,2,1,0:T(8,128)(2,1)S(1)} %copy-done.123), channel_id=1, source_target_pairs={{0,1},{2,3},{4,5},{6,7},{8,9},{10,11},{12,13},{14,15},{16,17},{18,... | collective-permute-start | bytes 147464 | tf_op jit(solution)/shard_map/ppermute | solution.py:22
  549.3 205.5 %collective-permute-start.7 = (bf16[2,1,64,192]{3,2,1,0:T(8,128)(2,1)}, bf16[2,1,64,192]{3,2,1,0:T(8,128)(2,1)}, u32[]{:S(2)}, u32[]{:S(2)}) collective-permute-start(bf16[2,1,64,192]{3,2,1,0:T(8,128)(2,1)} %get-tuple-element.165), channel_id=1, source_target_pairs={{1,0},{3,2},{5,4},{7,6},{9,8},{11,10},{13,12},{15,14},{17,16},{19,... | collective-permute-start | bytes 147464 | tf_op jit(solution)/shard_map/ppermute | solution.py:23
  550.6 11.2 %collective-permute-start.22 = (bf16[2,1,64,192]{3,2,1,0:T(8,128)(2,1)S(1)}, bf16[2,1,64,192]{3,2,1,0:T(8,128)(2,1)S(1)}, u32[]{:S(2)}, u32[]{:S(2)}) collective-permute-start(bf16[2,1,64,192]{3,2,1,0:T(8,128)(2,1)S(1)} %get-tuple-element.155), channel_id=1, source_target_pairs={{0,1},{2,3},{4,5},{6,7},{8,9},{10,11},{12,13},{14,15},{16,17},{18,... | collective-permute-start | bytes 147464 | tf_op jit(solution)/shard_map/ppermute | solution.py:22
  555.8 10.6 %collective-permute-start.23 = (bf16[2,1,64,192]{3,2,1,0:T(8,128)(2,1)S(1)}, bf16[2,1,64,192]{3,2,1,0:T(8,128)(2,1)S(1)}, u32[]{:S(2)}, u32[]{:S(2)}) collective-permute-start(bf16[2,1,64,192]{3,2,1,0:T(8,128)(2,1)S(1)} %get-tuple-element.154), channel_id=1, source_target_pairs={{1,0},{3,2},{5,4},{7,6},{9,8},{11,10},{13,12},{15,14},{17,16},{19,... | collective-permute-start | bytes 147464 | tf_op jit(solution)/shard_map/ppermute | solution.py:23
  561.8 20.7 %collective-permute-start.18 = (bf16[2,1,64,192]{3,2,1,0:T(8,128)(2,1)S(1)}, bf16[2,1,64,192]{3,2,1,0:T(8,128)(2,1)S(1)}, u32[]{:S(2)}, u32[]{:S(2)}) collective-permute-start(bf16[2,1,64,192]{3,2,1,0:T(8,128)(2,1)S(1)} %get-tuple-element.151), channel_id=1, source_target_pairs={{0,1},{2,3},{4,5},{6,7},{8,9},{10,11},{12,13},{14,15},{16,17},{18,... | collective-permute-start | bytes 147464 | tf_op jit(solution)/shard_map/ppermute | solution.py:22
  566.3 17.5 %collective-permute-start.19 = (bf16[2,1,64,192]{3,2,1,0:T(8,128)(2,1)S(1)}, bf16[2,1,64,192]{3,2,1,0:T(8,128)(2,1)S(1)}, u32[]{:S(2)}, u32[]{:S(2)}) collective-permute-start(bf16[2,1,64,192]{3,2,1,0:T(8,128)(2,1)S(1)} %get-tuple-element.150), channel_id=1, source_target_pairs={{1,0},{3,2},{5,4},{7,6},{9,8},{11,10},{13,12},{15,14},{17,16},{19,... | collective-permute-start | bytes 147464 | tf_op jit(solution)/shard_map/ppermute | solution.py:23
  582.5 20.4 %collective-permute-start.15 = (bf16[2,1,64,192]{3,2,1,0:T(8,128)(2,1)S(1)}, bf16[2,1,64,192]{3,2,1,0:T(8,128)(2,1)S(1)}, u32[]{:S(2)}, u32[]{:S(2)}) collective-permute-start(bf16[2,1,64,192]{3,2,1,0:T(8,128)(2,1)S(1)} %get-tuple-element.152), channel_id=1, source_target_pairs={{1,0},{3,2},{5,4},{7,6},{9,8},{11,10},{13,12},{15,14},{17,16},{19,... | collective-permute-start | bytes 147464 | tf_op jit(solution)/shard_map/ppermute | solution.py:23
  583.8 20.4 %collective-permute-start.14 = (bf16[2,1,64,192]{3,2,1,0:T(8,128)(2,1)S(1)}, bf16[2,1,64,192]{3,2,1,0:T(8,128)(2,1)S(1)}, u32[]{:S(2)}, u32[]{:S(2)}) collective-permute-start(bf16[2,1,64,192]{3,2,1,0:T(8,128)(2,1)S(1)} %get-tuple-element.153), channel_id=1, source_target_pairs={{0,1},{2,3},{4,5},{6,7},{8,9},{10,11},{12,13},{14,15},{16,17},{18,... | collective-permute-start | bytes 147464 | tf_op jit(solution)/shard_map/ppermute | solution.py:22
  602.9 151.9 %collective-permute-start.6 = (bf16[2,1,64,192]{3,2,1,0:T(8,128)(2,1)}, bf16[2,1,64,192]{3,2,1,0:T(8,128)(2,1)S(1)}, u32[]{:S(2)}, u32[]{:S(2)}) collective-permute-start(bf16[2,1,64,192]{3,2,1,0:T(8,128)(2,1)} %get-tuple-element.164), channel_id=1, source_target_pairs={{0,1},{2,3},{4,5},{6,7},{8,9},{10,11},{12,13},{14,15},{16,17},{18,... | collective-permute-start | bytes 147464 | tf_op jit(solution)/shard_map/ppermute | solution.py:22
  604.2 26.6 %collective-permute-start.3 = (bf16[2,1,64,192]{3,2,1,0:T(8,128)(2,1)S(1)}, bf16[2,1,64,192]{3,2,1,0:T(8,128)(2,1)S(1)}, u32[]{:S(2)}, u32[]{:S(2)}) collective-permute-start(bf16[2,1,64,192]{3,2,1,0:T(8,128)(2,1)S(1)} %get-tuple-element.163), channel_id=1, source_target_pairs={{1,0},{3,2},{5,4},{7,6},{9,8},{11,10},{13,12},{15,14},{17,16},{19,... | collective-permute-start | bytes 147464 | tf_op jit(solution)/shard_map/ppermute | solution.py:23
  617.7 13.1 %collective-permute-start.2 = (bf16[2,1,64,192]{3,2,1,0:T(8,128)(2,1)S(1)}, bf16[2,1,64,192]{3,2,1,0:T(8,128)(2,1)S(1)}, u32[]{:S(2)}, u32[]{:S(2)}) collective-permute-start(bf16[2,1,64,192]{3,2,1,0:T(8,128)(2,1)S(1)} %get-tuple-element.162), channel_id=1, source_target_pairs={{0,1},{2,3},{4,5},{6,7},{8,9},{10,11},{12,13},{14,15},{16,17},{18,... | collective-permute-start | bytes 147464 | tf_op jit(solution)/shard_map/ppermute | solution.py:22
  640.1 232.0 %reduce-scatter.15.cloned.1.call-start = ((), (), s32[]{:S(2)}) async-start(), calls=%async_computation.6 | async-start | bytes 5308416 | tf_op jit(solution)/shard_map/reduce_scatter | solution.py:234
  752.2 131.5 %reduce-scatter.21.cloned.1.call-start = ((), (), s32[]{:S(2)}) async-start(), calls=%async_computation.12 | async-start | bytes 147456
  795.1 89.4 %reduce-scatter.19.cloned.1.call-start = ((), (), s32[]{:S(2)}) async-start(), calls=%async_computation.11 | async-start | bytes 147456
  796.7 88.8 %reduce-scatter.25.cloned.1.call-start = ((), (), s32[]{:S(2)}) async-start(), calls=%async_computation.14 | async-start | bytes 147456
  799.6 86.7 %reduce-scatter.23.cloned.1.call-start = ((), (), s32[]{:S(2)}) async-start(), calls=%async_computation.13 | async-start | bytes 147456
  804.0 188.1 %all-reduce.20.cloned.1.call-start = ((), (), s32[]{:S(2)}) async-start(), calls=%async_computation.15 | async-start | bytes 9437184 | tf_op jit(solution)/shard_map/psum | solution.py:238
  (191 other events, 1465.5 us)
Sparse Core Ops, SparseCore 0:
  10.7 34.7 all-gather.19
  47.0 31.6 all-gather.17
  101.1 44.9 all-gather.15
  640.2 47.8 reduce-scatter.16
  752.3 49.2 reduce-scatter.14
  803.7 9.9 reduce-scatter.20
  815.9 9.9 reduce-scatter.18
  828.2 9.9 reduce-scatter.24
  840.4 9.9 reduce-scatter.22
  872.3 119.7 all-reduce.19
where the time goes:
time: 1010 us; the launch traced here: 1000 us
  matrix products  517 us (51%)
  blocking collectives  159 us (16%)
  other arithmetic  118 us (12%)
  local copies, waits for them, and re-layouts  79.2 us (8%)
  starting transfers between devices  67.5 us (7%)
  waiting for transfers between devices  45.6 us (5%)
  between operations  17.9 us (2%)
    dot_general x54, matrix products, conv_back(): jnp.einsum('bhwd,cd->bhwc', window, kernel[row_tap, col_tap], preferred_e...  243 us
    dot_general x54, matrix products, conv_apply(): jnp.einsum('bhwc,cd->bhwd', window, kernel[row_tap, col_tap], preferred_e...  236 us
    psum x1, blocking collectives, on_device(): lax.psum((kernel_piece, gain_piece, jnp.concatenate([bias_piece, mod_piec...  59 us
    ppermute x12, starting transfers between devices, extended(): before = lax.ppermute(last, axis, up)  50.6 us
    psum x1, waiting for transfers between devices, on_device(): lax.psum((kernel_piece, gain_piece, jnp.concatenate([bias_piece, mod_piec...  44.7 us
    all_gather x3, blocking collectives, on_device(): lax.all_gather(affine_weight[network], 'fsdp', axis=0, tiled=True)  41.4 us
    dot_general x36, matrix products, kernel_grad(): jnp.einsum('bhwc,bhwd->cd', window, gradient, preferred_element_type=jnp....  34.8 us
    concatenate x12, other arithmetic, extended(): x = jnp.concatenate([before, x, after], axis=dim)  22.8 us
  transfers between devices with their start and end apart: 34, of which 1 were waited for; matrix products, arithmetic and copies ran while one was open for 41% of the time, Pallas kernels for 0%

commit v1 on v0

v1 whole, which is shorter than its diff:
```python
import functools
import types

import jax
import jax.numpy as jnp
from jax import lax
from jax.experimental import pallas as pl
from jax.experimental.pallas import tpu as pltpu
from jax.sharding import PartitionSpec as P

GROUPS = 32
EPSILON = 1e-05
LANES = 128
CHUNK = 64
MESH = pl.DeviceIdType.MESH
F32 = jnp.float32
BF16 = jnp.bfloat16

MU0, R0, G0, G1, B1, B2, B3, SC1, SH, SGY, MU1, R1, SUMH = range(13)
PA0, PB0, PMU0, PBIAS, PA1, PB1, PMU1, PDA, PDB, PDC = range(10)


def settings(dp_size, fsdp_size, nets, slots, rows, width, chans, embed_rows):
    g = types.SimpleNamespace()
    g.dp, g.f, g.nets, g.s, g.r, g.w, g.c, g.ef = (
        dp_size, fsdp_size, nets, slots, rows, width, chans, embed_rows,
    )
    g.np = rows // 2
    g.u = min(4, g.np)
    g.px = g.np * LANES
    g.count = float(rows * fsdp_size * width * (chans // GROUPS))
    g.pixels = float(rows * fsdp_size * width)
    g.bits = dp_size.bit_length() - 1
    g.shard = chans // fsdp_size
    g.low_rows = 9 * g.shard
    g.high_rows = -(-g.low_rows // 16) * 8
    unit = 8 << (g.bits - 1)
    g.pack = -(-(g.low_rows + g.high_rows) // unit) * unit
    g.wide = max(2 * chans, embed_rows)
    g.stages = 2 * g.bits
    return g


def kernel_body(
    g,
    x_h, gy_h, w_h, aff, emb, gb, keep,
    y_h, dx_h, cg_h, ag_h, sg,
    rx, rg, xc, gc, xa0, xa1, xg, hb, xe, hbuf, dub, wraw, wf, wb, gacc, pk, r0b, ryb, rbb,
    ys, cgs, ags, ex1, ex2, sb, acc, rowt, prm,
    lx, lg, ysem, hs, hr, es, er, wl, wys, wyr, wcs, wcr, cs, cr, ss, sr, osem,
):
    me = lax.axis_index("fsdp")
    dp = lax.axis_index("dp")
    C, NP, F, S, R = g.c, g.np, g.f, g.s, g.r
    PX = g.px

    def net_of(i):
        return (2 * i) % g.nets

    def peer(df):
        return (me + df) % F

    def source(df):
        return (me + F - df) % F

    def bit(b):
        return (dp // (1 << b)) % 2

    def partner(b):
        return dp + (1 << b) * (1 - 2 * bit(b))

    def remote(src, dst, send, recv, where):
        return pltpu.make_async_remote_copy(
            src_ref=src, dst_ref=dst, send_sem=send, recv_sem=recv,
            device_id=where, device_id_type=MESH,
        )

    def tile(t):
        if isinstance(t, int):
            return pl.ds(t * LANES, LANES)
        return pl.ds(pl.multiple_of(t * LANES, LANES), LANES)

    lane = lax.broadcasted_iota(jnp.int32, (C, LANES), 1)
    low_lanes = lane < g.w
    top = (me > 0).astype(jnp.int32)
    bottom = (me < F - 1).astype(jnp.int32)
    edge_ok = jnp.where(low_lanes, top, bottom) > 0


    def halo_copy(i, s, t, down):
        src = (x_h, gy_h)[t]
        n = net_of(i)
        if down:
            return remote(
                src.at[n, s, pl.ds(R - 2, 2)], hb.at[i, s, t, 0],
                hs.at[i, s, t, 1], hr.at[i, s, t, 1], {"fsdp": (me + 1) % F},
            )
        return remote(
            src.at[n, s, pl.ds(0, 2)], hb.at[i, s, t, 1],
            hs.at[i, s, t, 0], hr.at[i, s, t, 0], {"fsdp": (me + F - 1) % F},
        )

    def halo_start(i, s, t):
        @pl.when(me > 0)
        def _():
            halo_copy(i, s, t, False).start()

        @pl.when(me < F - 1)
        def _():
            halo_copy(i, s, t, True).start()

    def halo_take(i, s, t):
        @pl.when(me > 0)
        def _():
            halo_copy(i, s, t, True).wait_recv()

        @pl.when(me < F - 1)
        def _():
            halo_copy(i, s, t, False).wait_recv()

    def halo_sent(i, s, t):
        @pl.when(me > 0)
        def _():
            halo_copy(i, s, t, False).wait_send()

        @pl.when(me < F - 1)
        def _():
            halo_copy(i, s, t, True).wait_send()

    def row_copy(i, e, s, df, who):
        ref = ex1.at[i, s, who] if e == 0 else ex2.at[i, e - 1, s, who]
        return remote(ref, ref, es.at[i, e, s, df], er.at[i, e, s, df], {"fsdp": peer(df)})

    def rows_start(i, e, s):
        for df in range(1, F):
            row_copy(i, e, s, df, me).start()

    def rows_take(i, e, s):
        for df in range(1, F):
            row_copy(i, e, s, df, source(df)).wait_recv()
        parts = [ex1[i, s, f] if e == 0 else ex2[i, e - 1, s, f] for f in range(F)]
        total = parts[0]
        for part in parts[1:]:
            total = total + part
        return total

    mine = dp % 2
    sibling = partner(0)

    def weight_copy(i, df, who):
        return remote(
            w_h.at[net_of(i), mine], wraw.at[i, who, mine],
            wys.at[i, df], wyr.at[i, df], {"fsdp": peer(df)},
        )

    def weight_share(i, df, kind):
        ref = wraw.at[i, source(df), kind]
        return remote(ref, ref, wcs.at[i, df], wcr.at[i, df], {"dp": sibling})

    def weight_local(i):
        return pltpu.make_async_copy(w_h.at[net_of(i)], wraw.at[i, me], wl.at[i])

    def weights_start(i):
        for df in range(1, F):
            weight_copy(i, df, me).start()
        weight_local(i).start()

    def weights_forward(i):
        for df in range(1, F):
            weight_copy(i, df, source(df)).wait_recv()
            weight_share(i, df, mine).start()

    def weights_take(i):
        weight_local(i).wait()
        for df in range(1, F):
            weight_share(i, df, 1 - mine).wait_recv()

    def net_start(i):
        for t in range(2):
            for s in range(S):
                halo_start(i, s, t)
        weights_start(i)


    def part(b):
        return g.pack >> (b + 1)

    def base(b):
        offset = 0
        for b2 in range(b + 1):
            offset = offset + bit(b2) * part(b2)
        return offset

    def rows_at(offset, size):
        if not isinstance(offset, int):
            offset = pl.multiple_of(offset, 8)
        return pl.ds(offset, size)

    def away(b):
        return rows_at(base(b - 1) + (1 - bit(b)) * part(b), part(b))

    def home(b):
        return rows_at(base(b), part(b))

    def region(b):
        return sum(part(b2) for b2 in range(1, b))

    last_bit = g.bits - 1

    def stage_copies(m, k, t):
        if t == 0:
            return [(
                remote(pk.at[k, :, away(0)], r0b.at[k], cs.at[m, k, 0, 0], cr.at[m, k, 0, 0], {"dp": partner(0)}),
                None,
            )]
        if t == 1:
            return [
                (
                    remote(
                        pk.at[k, peer(df), home(0)], ryb.at[k, df - 1],
                        cs.at[m, k, 1, df - 1], cr.at[m, k, 1, df - 1], {"fsdp": peer(df)},
                    ),
                    None,
                )
                for df in range(1, F)
            ]
        if t <= g.bits:
            b = t - 1
            rows = home(b - 1) if b == last_bit else away(b)
            size = part(b - 1) if b == last_bit else part(b)
            return [(
                remote(
                    pk.at[k, me, rows], rbb.at[k, pl.ds(region(b), size)],
                    cs.at[m, k, t, 0], cr.at[m, k, t, 0], {"dp": partner(b)},
                ),
                None,
            )]
        b = 2 * g.bits - 1 - t
        own = pk.at[k, me, home(b)]
        other = pk.at[k, me, away(b)]
        where = {"dp": partner(b)}
        return [(
            remote(own, own, cs.at[m, k, t, 0], cr.at[m, k, t, 0], where),
            remote(own, other, cs.at[m, k, t, 0], cr.at[m, k, t, 0], where),
        )]

    def add_rows(dst, dst_start, src, src_start, size):
        step = part(last_bit - 1)

        def body(j, carry):
            a = rows_at(dst_start + j * step, step)
            b = rows_at(src_start + j * step, step)
            dst[a, :] = dst[a, :] + src[b, :]
            return carry

        lax.fori_loop(0, size // step, body, 0)

    def stage_start(m, k, t):
        for copy, _ in stage_copies(m, k, t):
            copy.start()

    def stage_finish(m, k, t):
        for copy, received in stage_copies(m, k, t):
            copy.wait_send()
            (received or copy).wait_recv()
        if t == 0:
            for f in range(F):
                add_rows(pk.at[k, f], base(0), r0b.at[k, f], 0, part(0))
        elif t == 1:
            for df in range(1, F):
                add_rows(pk.at[k, me], base(0), ryb.at[k, df - 1], 0, part(0))
        elif t <= g.bits:
            b = t - 1
            kept = last_bit - 1 if b == last_bit else b
            add_rows(pk.at[k, me], base(kept), rbb.at[k], region(b), part(kept))

    def small_copy(m, b, received):
        size = 1 << b
        start = (dp // size) * size
        there = start + size * (1 - 2 * bit(b))
        own = sb.at[m, pl.ds(start, size)]
        dst = sb.at[m, pl.ds(there, size)] if received else own
        return remote(own, dst, ss.at[m, b], sr.at[m, b], {"dp": partner(b)})

    round_at = [1] + [b + 2 for b in range(1, g.bits)]

    def tick(i, t):
        @pl.when(i > 0)
        def _():
            m = i - 1
            for k in range(2):
                stage_finish(m, k, t - 1)
            for b in range(g.bits):
                ends = round_at[b + 1] if b + 1 < g.bits else round_at[b] + 1
                if t == ends:
                    small_copy(m, b, False).wait_send()
                    small_copy(m, b, True).wait_recv()
            for b in range(g.bits):
                if t == round_at[b]:
                    small_copy(m, b, False).start()
            if t < g.stages:
                for k in range(2):
                    stage_start(m, k, t)
            else:
                finish_large(m)
            if t == round_at[-1] + 1:
                finish_small(m)

    def finish_small(m):
        total = sb[m, 0, 0:8, 0:C]
        for d in range(1, g.dp):
            total = total + sb[m, d, 0:8, 0:C]
        sg[m] = total
        block = sb[m, :, 8:16, :].reshape(g.dp * 8, g.wide)
        index = lax.broadcasted_iota(jnp.int32, (g.dp * 8, g.ef), 0) & 7
        left = jnp.where(index < S, block[:, : g.ef], 0.0).astype(BF16)
        right = pltpu.roll(block[:, : 2 * C], g.dp * 8 - S, 0).astype(BF16)

        @pl.when(m > 0)
        def _():
            pltpu.make_async_copy(ags, ag_h.at[m], osem.at[2]).wait()

        ags[...] = lax.dot_general(left, right, (((0,), (0,)), ((), ())), preferred_element_type=F32)
        pltpu.make_async_copy(ags, ag_h.at[m], osem.at[2]).start()

    def finish_large(m):
        for k in range(2):
            out = pltpu.make_async_copy(cgs.at[k], cg_h.at[m, k], osem.at[k])

            @pl.when(m > 0)
            def _():
                out.wait()

            cgs[k, :, 0:LANES] = pk[k, me, 0 : g.low_rows, :]
            split = g.low_rows - g.high_rows
            cgs[k, 0 : g.high_rows, LANES:C] = pk[k, me, g.low_rows : g.low_rows + g.high_rows, 0 : C - LANES]
            cgs[k, g.high_rows : g.low_rows, LANES:C] = pk[k, me, g.low_rows : g.low_rows + split, CHUNK : CHUNK + C - LANES]
            out.start()

    def pack_start(m):
        for k in range(2):
            for f in range(F):
                for tap in range(9):
                    first, last = tap * g.shard, (tap + 1) * g.shard
                    c0 = tap * C + f * g.shard
                    pk[k, f, first:last, :] = gacc[k, c0 : c0 + g.shard, 0:LANES]
                    for lo, hi, lanes in ((0, g.high_rows, 0), (g.high_rows, g.low_rows, CHUNK)):
                        a, b = max(first, lo), min(last, hi)
                        if a < b:
                            at = g.low_rows + a - lo
                            pk[k, f, at : at + b - a, lanes : lanes + C - LANES] = gacc[
                                k, c0 + a - first : c0 + b - first, LANES:C
                            ]
            stage_start(m, k, 0)


    def shifted(v):
        col = lax.broadcasted_iota(jnp.int32, v.shape, 1) & (g.w - 1)
        left = jnp.where(col == 0, 0.0, pltpu.roll(v, 1, 1))
        right = jnp.where(col == g.w - 1, 0.0, pltpu.roll(v, LANES - 1, 1))
        return left, v, right

    def put(buf, s, rows, t, v):
        for j, moved in enumerate(shifted(v)):
            buf[s, j, rows, tile(t)] = moved.astype(BF16)

    def put_edges(buf, s, first_edge, second_edge):
        near = shifted(first_edge)
        far = None if second_edge is None else shifted(second_edge)
        for j in range(3):
            first = buf[s, j, :, tile(1)].astype(F32)
            last = buf[s, j, :, tile(NP)].astype(F32)
            buf[s, j, :, tile(0)] = jnp.where(low_lanes, near[j], pltpu.roll(last, g.w, 1)).astype(BF16)
            buf[s, j, :, tile(NP + 1)] = jnp.where(low_lanes, pltpu.roll(first, g.w, 1), near[j]).astype(BF16)
            if far is not None:
                buf[s, j, :, tile(NP + 2)] = jnp.where(low_lanes, far[j], last).astype(BF16)
                buf[s, j, :, tile(NP + 3)] = near[j].astype(BF16)
                buf[s, j, :, tile(NP + 4)] = jnp.where(low_lanes, first, far[j]).astype(BF16)

    def windows(buf, s, back, edge):
        pieces = []
        for i in range(3):
            for j in range(3):
                ti, tj = (2 - i, 2 - j) if back else (i, j)
                piece = buf[s, tj, :, ti * LANES : ti * LANES + PX]
                if edge:
                    piece = jnp.concatenate([piece, buf[s, tj, :, tile(NP + 2 + ti)]], axis=1)
                pieces.append(piece)
        return jnp.concatenate(pieces, axis=0)

    def chunks():
        return [pl.ds(c0, CHUNK) for c0 in range(0, C, CHUNK)]

    def over_tiles(body):
        def step(block, carry):
            body([block * g.u + u for u in range(g.u)])
            return carry

        lax.fori_loop(0, NP // g.u, step, 0)

    def clear(count):
        for k in range(count):
            acc[k] = jnp.zeros((C, LANES), F32)

    def total_row(k):
        return jnp.sum(acc[k].T, axis=0, keepdims=True)

    def group_rows(rows):
        high = rows.astype(BF16)
        rest = rows - high.astype(F32)
        middle = rest.astype(BF16)
        low = (rest - middle.astype(F32)).astype(BF16)
        a = lax.broadcasted_iota(jnp.int32, (C, C), 0) // (C // GROUPS)
        b = lax.broadcasted_iota(jnp.int32, (C, C), 1) // (C // GROUPS)
        same = jnp.where(a == b, 1.0, 0.0).astype(BF16)
        three = jnp.dot(jnp.concatenate([high, middle, low], axis=0).astype(BF16), same, preferred_element_type=F32)
        n = rows.shape[0]
        return three[0:n] + three[n : 2 * n] + three[2 * n : 3 * n]

    def stack(*rows):
        fill = 8 - len(rows)
        return jnp.concatenate(list(rows) + [jnp.zeros((fill, C), F32)] * (fill > 0), axis=0)

    def spread(s, k, row):
        prm[s, k] = jnp.broadcast_to(row, (LANES, C)).T

    def save(s, k, row):
        rowt[s, k : k + 1, :] = row

    def row(s, k):
        return rowt[s, k : k + 1, :]

    def moments(total):
        grouped = group_rows(total)
        mean = grouped[0:1] / g.count
        variance = grouped[1:2] / g.count - mean * mean
        return mean, lax.rsqrt(variance + EPSILON)

    def slope_twice(w, t):
        return (1.0 + t) * (1.0 + w * (1.0 - t))

    def pair(buf, s, q):
        return jnp.concatenate([buf[s, q], buf[s, q + NP]], axis=0)

    def pixels(s):
        return jnp.concatenate([rg[s, h] for q in range(NP) for h in (q, q + NP)], axis=0)


    def read_phase(i, s):
        n = net_of(i)
        kf = keep[s]
        pltpu.make_async_copy(x_h.at[n, s], rx.at[s], lx.at[s]).wait()
        pltpu.make_async_copy(gy_h.at[n, s], rg.at[s], lg.at[s]).wait()
        clear(3)

        def body(qs):
            for q in qs:
                xc[s, :, tile(q)] = pair(rx, s, q).T
                gc[s, :, tile(q)] = (pair(rg, s, q).T.astype(F32) * kf).astype(BF16)
            for rows in chunks():
                a0, a1, a2 = acc[0, rows], acc[1, rows], acc[2, rows]
                for q in qs:
                    xf = xc[s, rows, tile(q)].astype(F32)
                    a0 = a0 + xf
                    a1 = a1 + xf * xf
                    gf = gc[s, rows, tile(q)].astype(F32)
                    a2 = a2 + gf
                    put(xg, s, rows, q + 1, gf)
                acc[0, rows], acc[1, rows], acc[2, rows] = a0, a1, a2

        over_tiles(body)
        eight = emb[n, s]
        ex1[i, s, me, 0:8] = stack(
            total_row(0), total_row(1), total_row(2),
            jnp.dot(eight, aff[n, 0], preferred_element_type=F32)[0:1],
            jnp.dot(eight, aff[n, 1], preferred_element_type=F32)[0:1],
        )
        ex1[i, s, me, 8:16] = gb[n]
        rows_start(i, 0, s)

    def edge_phase(i, s):
        kf = keep[s]
        halo_take(i, s, 0)
        halo_take(i, s, 1)
        for t in range(2):
            near = jnp.concatenate([hb[i, s, t, 0, 1], hb[i, s, t, 1, 0]], axis=0).T.astype(F32)
            far = jnp.concatenate([hb[i, s, t, 0, 0], hb[i, s, t, 1, 1]], axis=0).T.astype(F32)
            near = jnp.where(edge_ok, near, 0.0)
            far = jnp.where(edge_ok, far, 0.0)
            if t == 0:
                xe[s, 0] = near
                xe[s, 1] = far
            else:
                put_edges(xg, s, near * kf, far * kf)

    def weights_ready(i):
        for k in range(2):
            for tap in range(9):
                blocks = [wraw[i, f, k, tap] for f in range(F)]
                if g.shard % 16:
                    blocks = [b.astype(F32) for b in blocks]
                whole = jnp.concatenate(blocks, axis=0).astype(BF16)
                wb[k, :, tap * C : (tap + 1) * C] = whole
                wf[k, :, tap * C : (tap + 1) * C] = whole.T

    def first_phase(i, s):
        total = rows_take(i, 0, s)
        mean, inverse = moments(total[0:8])
        save(s, MU0, mean)
        save(s, R0, inverse)
        save(s, SGY, total[2:3])
        gain0, gain1 = total[8:9], total[9:10]
        save(s, G0, gain0)
        save(s, G1, gain1)
        save(s, B1, total[11:12])
        save(s, B2, total[12:13])
        save(s, B3, total[13:14])
        save(s, SC1, total[3:4] + total[14:15] + 1.0)
        save(s, SH, total[4:5] + total[15:16])
        scale = inverse * gain0
        spread(s, PA0, 0.5 * scale)
        spread(s, PB0, 0.5 * (total[10:11] - mean * scale))
        spread(s, PMU0, mean)
        spread(s, PBIAS, total[11:12])

        def act(xf, a, b):
            w = xf * a + b
            return w * jnp.tanh(w) + w

        def body(qs):
            for rows in chunks():
                a, b = prm[s, PA0, rows], prm[s, PB0, rows]
                for q in qs:
                    put(xa0, s, rows, q + 1, act(xc[s, rows, tile(q)].astype(F32), a, b))

        over_tiles(body)
        edges = [jnp.where(edge_ok, act(xe[s, t], prm[s, PA0], prm[s, PB0]), 0.0) for t in range(2)]
        put_edges(xa0, s, edges[0], edges[1])
        dub[s] = jnp.dot(wb[1], windows(xg, s, True, True), preferred_element_type=F32)

    def hidden_phase(i, s):
        hbuf[s] = jnp.dot(wf[0], windows(xa0, s, False, True), preferred_element_type=F32)
        clear(2)

        def body(qs):
            for rows in chunks():
                bias = prm[s, PBIAS, rows]
                a0, a1 = acc[0, rows], acc[1, rows]
                for q in qs:
                    h = hbuf[s, rows, tile(q)] + bias
                    hbuf[s, rows, tile(q)] = h
                    a0 = a0 + h
                    a1 = a1 + h * h
                acc[0, rows], acc[1, rows] = a0, a1

        over_tiles(body)
        hbuf[s, :, tile(NP)] = hbuf[s, :, tile(NP)] + prm[s, PBIAS]
        ex2[i, 0, s, me] = stack(total_row(0), total_row(1))
        rows_start(i, 1, s)

    def second_phase(i, s):
        total = rows_take(i, 1, s)
        mean, inverse = moments(total)
        save(s, MU1, mean)
        save(s, R1, inverse)
        save(s, SUMH, total[0:1])
        scale = inverse * row(s, G1)
        spread(s, PA1, 0.5 * scale * row(s, SC1))
        spread(s, PB1, 0.5 * (row(s, SH) + (row(s, B2) - mean * scale) * row(s, SC1)))
        spread(s, PMU1, mean)
        clear(2)

        def body(qs):
            for rows in chunks():
                a, b, mu = prm[s, PA1, rows], prm[s, PB1, rows], prm[s, PMU1, rows]
                a0, a1 = acc[0, rows], acc[1, rows]
                for q in qs:
                    h = hbuf[s, rows, tile(q)]
                    w = h * a + b
                    t = jnp.tanh(w)
                    put(xa1, s, rows, q + 1, w * t + w)
                    d = dub[s, rows, tile(q)] * slope_twice(w, t)
                    dub[s, rows, tile(q)] = d
                    a0 = a0 + d
                    a1 = a1 + d * (h - mu)
                acc[0, rows], acc[1, rows] = a0, a1

        over_tiles(body)
        w = hbuf[s, :, tile(NP)] * prm[s, PA1] + prm[s, PB1]
        t = jnp.tanh(w)
        put_edges(xa1, s, jnp.where(edge_ok, w * t + w, 0.0), None)
        dub[s, :, tile(NP)] = dub[s, :, tile(NP)] * slope_twice(w, t)
        ex2[i, 1, s, me] = stack(0.5 * total_row(0), 0.5 * total_row(1))
        rows_start(i, 2, s)

    def out_copy(i, s):
        return pltpu.make_async_copy(ys.at[s], y_h.at[net_of(i), s], ysem.at[s])

    def in_grad_copy(i, s):
        return pltpu.make_async_copy(ys.at[s], dx_h.at[net_of(i), s], ysem.at[s])

    def put_pixels(s, q, v):
        flat = v.astype(BF16).T
        ys[s, q] = flat[0 : g.w]
        ys[s, q + NP] = flat[g.w : 2 * g.w]

    def output_phase(i, s):
        kf = keep[s]
        spread(s, PBIAS, row(s, B3))
        branch = jnp.dot(wf[1], windows(xa1, s, False, False), preferred_element_type=F32)

        @pl.when(i > 0)
        def _():
            in_grad_copy(i, s).wait()

        for q in range(NP):
            v = branch[:, q * LANES : (q + 1) * LANES] + prm[s, PBIAS] + xc[s, :, tile(q)].astype(F32)
            put_pixels(s, q, v * kf)
        out_copy(i, s).start()

        @pl.when(i < 2)
        def _():
            o = jnp.dot(windows(xa1, s, False, False), pixels(s), preferred_element_type=F32)
            gacc[1] = gacc[1] + o * kf

    def hidden_grad_phase(i, s):
        total = rows_take(i, 2, s)
        s1, s2 = total[0:1], total[1:2] * row(s, R1)
        sc1, gain1, inverse, mean = row(s, SC1), row(s, G1), row(s, R1), row(s, MU1)
        grouped = group_rows(stack(gain1 * sc1 * s1, gain1 * sc1 * s2))
        m1, m2 = grouped[0:1] / g.count, grouped[1:2] / g.count
        a = inverse * sc1 * gain1
        b = -inverse * inverse * m2
        c = -inverse * m1 - mean * b
        spread(s, PDA, 0.5 * a)
        spread(s, PDB, b)
        spread(s, PDC, c)

        @pl.when(i < 2)
        def _():
            dscale = gain1 * s2 + row(s, B2) * s1
            here = sb.at[i, dp]
            here[1:2, 0:C] = here[1:2, 0:C] + sc1 * s2
            here[3:4, 0:C] = here[3:4, 0:C] + a * s1 + b * row(s, SUMH) + c * g.pixels
            here[4:5, 0:C] = here[4:5, 0:C] + sc1 * s1
            here[5:6, 0:C] = here[5:6, 0:C] + row(s, SGY)
            here[6:7, 0:C] = here[6:7, 0:C] + dscale
            here[7:8, 0:C] = here[7:8, 0:C] + s1
            modulation = jnp.concatenate([dscale, s1], axis=1).astype(BF16).astype(F32)
            for slot in range(S):
                @pl.when(s == slot)
                def _():
                    here[8 + slot : 9 + slot, 0 : g.ef] = emb[net_of(i), s].astype(F32)[0:1]
                    here[8 + S + slot : 9 + S + slot, 0 : 2 * C] = modulation

        def body(qs):
            for rows in chunks():
                a, b, c = prm[s, PDA, rows], prm[s, PDB, rows], prm[s, PDC, rows]
                for q in qs:
                    d = dub[s, rows, tile(q)] * a + hbuf[s, rows, tile(q)] * b + c
                    put(xg, s, rows, q + 1, d)
            for q in qs:
                flat = xg[s, 1, :, tile(q + 1)].T
                rg[s, q] = flat[0 : g.w]
                rg[s, q + NP] = flat[g.w : 2 * g.w]

        over_tiles(body)
        d = dub[s, :, tile(NP)] * prm[s, PDA] + hbuf[s, :, tile(NP)] * prm[s, PDB] + prm[s, PDC]
        put_edges(xg, s, jnp.where(edge_ok, d, 0.0), None)

    def input_grad_phase(i, s):
        hbuf[s, :, 0:PX] = jnp.dot(wb[0], windows(xg, s, True, False), preferred_element_type=F32)
        clear(2)

        def body(qs):
            for rows in chunks():
                a, b, mu = prm[s, PA0, rows], prm[s, PB0, rows], prm[s, PMU0, rows]
                a0, a1 = acc[0, rows], acc[1, rows]
                for q in qs:
                    xf = xc[s, rows, tile(q)].astype(F32)
                    w = xf * a + b
                    d = hbuf[s, rows, tile(q)] * slope_twice(w, jnp.tanh(w))
                    hbuf[s, rows, tile(q)] = d
                    a0 = a0 + d
                    a1 = a1 + d * (xf - mu)
                acc[0, rows], acc[1, rows] = a0, a1

        over_tiles(body)
        ex2[i, 2, s, me] = stack(0.5 * total_row(0), 0.5 * total_row(1))
        rows_start(i, 3, s)

    def weight_phase(i, s):
        gacc[0] = gacc[0] + jnp.dot(windows(xa0, s, False, False), pixels(s), preferred_element_type=F32)

    def last_phase(i, s):
        total = rows_take(i, 3, s)
        inverse, mean, gain0 = row(s, R0), row(s, MU0), row(s, G0)
        s3, s4 = total[0:1], total[1:2] * inverse
        grouped = group_rows(stack(gain0 * s3, gain0 * s4))
        m1, m2 = grouped[0:1] / g.count, grouped[1:2] / g.count
        b = -inverse * inverse * m2
        spread(s, PA1, 0.5 * inverse * gain0)
        spread(s, PB1, b)
        spread(s, PMU1, -inverse * m1 - mean * b)

        @pl.when(i < 2)
        def _():
            here = sb.at[i, dp]
            here[0:1, 0:C] = here[0:1, 0:C] + s4
            here[2:3, 0:C] = here[2:3, 0:C] + s3

        out_copy(i, s).wait()

        def body(qs):
            for q in qs:
                xf = xc[s, :, tile(q)].astype(F32)
                v = hbuf[s, :, tile(q)] * prm[s, PA1] + xf * prm[s, PB1] + prm[s, PMU1]
                put_pixels(s, q, v + gc[s, :, tile(q)].astype(F32))

        over_tiles(body)
        in_grad_copy(i, s).start()


    def slots(phase, i):
        def step(s, carry):
            phase(i, s)
            return carry

        lax.fori_loop(0, S, step, 0)

    def load_x(i):
        for s in range(S):
            pltpu.make_async_copy(x_h.at[net_of(i), s], rx.at[s], lx.at[s]).start()

    def load_gy(i):
        for s in range(S):
            pltpu.make_async_copy(gy_h.at[net_of(i), s], rg.at[s], lg.at[s]).start()

    load_x(0)
    load_gy(0)
    pk[:, :, g.low_rows + g.high_rows :, :] = jnp.zeros((2, F, g.pack - g.low_rows - g.high_rows, LANES), F32)

    @pl.when(me == 0)
    def _():
        hb[:, :, :, 0] = jnp.zeros(hb.shape[:3] + hb.shape[4:], BF16)

    @pl.when(me == F - 1)
    def _():
        hb[:, :, :, 1] = jnp.zeros(hb.shape[:3] + hb.shape[4:], BF16)

    barrier = pltpu.get_barrier_semaphore()
    for df in range(1, F):
        pl.semaphore_signal(barrier, inc=1, device_id={"fsdp": peer(df)}, device_id_type=MESH)
    for b in range(g.bits):
        pl.semaphore_signal(barrier, inc=1, device_id={"dp": partner(b)}, device_id_type=MESH)
    pl.semaphore_wait(barrier, F - 1 + g.bits)
    net_start(0)

    def network(i, carry):
        @pl.when(i < 2)
        def _():
            net_start(i + 1)
            sb[i, dp] = jnp.zeros((16, g.wide), F32)
            gacc[...] = jnp.zeros(gacc.shape, F32)

        slots(read_phase, i)

        @pl.when(i < 2)
        def _():
            load_x(i + 1)

        slots(edge_phase, i)
        tick(i, 1)
        weights_forward(i)
        weights_take(i)
        weights_ready(i)
        slots(first_phase, i)
        slots(hidden_phase, i)
        slots(second_phase, i)
        tick(i, 2)
        slots(output_phase, i)
        tick(i, 3)
        slots(hidden_grad_phase, i)
        tick(i, 4)
        slots(input_grad_phase, i)
        tick(i, 5)

        @pl.when(i < 2)
        def _():
            slots(weight_phase, i)
            load_gy(i + 1)

        slots(last_phase, i)
        for t in range(6, g.stages + 1):
            tick(i, t)

        @pl.when(i < 2)
        def _():
            pack_start(i)

        return carry

    lax.fori_loop(0, 3, network, 0)


    def drain(i, carry):
        for s in range(S):
            for t in range(2):
                halo_sent(i, s, t)
            for e in range(4):
                for df in range(1, F):
                    row_copy(i, e, s, df, me).wait_send()
        for df in range(1, F):
            weight_copy(i, df, me).wait_send()
            weight_share(i, df, mine).wait_send()
        return carry

    lax.fori_loop(0, 3, drain, 0)
    for s in range(S):
        in_grad_copy(2, s).wait()
    for k in range(2):
        pltpu.make_async_copy(cgs.at[k], cg_h.at[1, k], osem.at[k]).wait()
    pltpu.make_async_copy(ags, ag_h.at[1], osem.at[2]).wait()


def on_device(
    block_input, embedding, out_cotangent, conv_weights, affine_weight, gains, biases, counts
):
    nets, slots, rows, width, chans = block_input.shape
    fsdp = lax.axis_size("fsdp")
    dp = lax.axis_size("dp")
    me = lax.axis_index("fsdp")
    embed_rows = affine_weight.shape[1]
    g = settings(dp, fsdp, nets, slots, rows, width, chans, embed_rows)

    keep = (jnp.arange(slots) < counts[0]).astype(F32)
    weights = conv_weights.reshape(nets, 2, 9, g.shard, chans)
    affine = affine_weight.reshape(nets, embed_rows, 2, chans).transpose(0, 2, 1, 3)
    embed = lax.dynamic_slice_in_dim(embedding, me * embed_rows, embed_rows, 2)
    embed = jnp.broadcast_to(embed[:, :, None, :], (nets, slots, 16, embed_rows))
    vectors = jnp.concatenate([gains, biases], axis=1).astype(F32)
    vectors = lax.dynamic_update_slice_in_dim(
        jnp.zeros((nets, 8, chans), F32), vectors, me * g.shard, 2
    )

    tiles = (g.np + 1) * LANES
    dma = pltpu.SemaphoreType.DMA
    scratch = [
        pltpu.VMEM((slots, rows, width, chans), BF16),
        pltpu.VMEM((slots, rows, width, chans), BF16),
        pltpu.VMEM((slots, chans, g.px), BF16),
        pltpu.VMEM((slots, chans, g.px), BF16),
        pltpu.VMEM((slots, 3, chans, (g.np + 5) * LANES), BF16),
        pltpu.VMEM((slots, 3, chans, (g.np + 2) * LANES), BF16),
        pltpu.VMEM((slots, 3, chans, (g.np + 5) * LANES), BF16),
        pltpu.VMEM((3, slots, 2, 2, 2, width, chans), BF16),
        pltpu.VMEM((slots, 2, chans, LANES), F32),
        pltpu.VMEM((slots, chans, tiles), F32),
        pltpu.VMEM((slots, chans, tiles), F32),
        pltpu.VMEM((3, fsdp, 2, 9, g.shard, chans), BF16),
        pltpu.VMEM((2, chans, 9 * chans), BF16),
        pltpu.VMEM((2, chans, 9 * chans), BF16),
        pltpu.VMEM((2, 9 * chans, chans), F32),
        pltpu.VMEM((2, fsdp, g.pack, LANES), F32),
        pltpu.VMEM((2, fsdp, g.pack // 2, LANES), F32),
        pltpu.VMEM((2, fsdp - 1, g.pack // 2, LANES), F32),
        pltpu.VMEM((2, g.pack // 2, LANES), F32),
        pltpu.VMEM((slots, rows, width, chans), BF16),
        pltpu.VMEM((2, g.low_rows, chans), F32),
        pltpu.VMEM((embed_rows, 2 * chans), F32),
        pltpu.VMEM((3, slots, fsdp, 16, chans), F32),
        pltpu.VMEM((3, 3, slots, fsdp, 8, chans), F32),
        pltpu.VMEM((2, dp, 16, g.wide), F32),
        pltpu.VMEM((3, chans, LANES), F32),
        pltpu.VMEM((slots, 16, chans), F32),
        pltpu.VMEM((slots, 10, chans, LANES), F32),
        dma((slots,)),
        dma((slots,)),
        dma((slots,)),
        dma((3, slots, 2, 2)),
        dma((3, slots, 2, 2)),
        dma((3, 4, slots, fsdp)),
        dma((3, 4, slots, fsdp)),
        dma((3,)),
        dma((3, fsdp)),
        dma((3, fsdp)),
        dma((3, fsdp)),
        dma((3, fsdp)),
        dma((2, 2, g.stages, fsdp)),
        dma((2, 2, g.stages, fsdp)),
        dma((2, g.bits)),
        dma((2, g.bits)),
        dma((3,)),
    ]
    hbm = pl.BlockSpec(memory_space=pl.ANY)
    vmem = pl.BlockSpec(memory_space=pltpu.VMEM)
    smem = pl.BlockSpec(memory_space=pltpu.SMEM)
    block_output, input_grad, conv_grads, affine_grad, sums = pl.pallas_call(
        functools.partial(kernel_body, g),
        out_shape=(
            jax.ShapeDtypeStruct(block_input.shape, BF16),
            jax.ShapeDtypeStruct(block_input.shape, BF16),
            jax.ShapeDtypeStruct((2, 2, g.low_rows, chans), F32),
            jax.ShapeDtypeStruct((2, embed_rows, 2 * chans), F32),
            jax.ShapeDtypeStruct((2, 8, chans), F32),
        ),
        in_specs=[hbm, hbm, hbm, vmem, vmem, vmem, smem],
        out_specs=(hbm, hbm, hbm, hbm, vmem),
        scratch_shapes=scratch,
        compiler_params=pltpu.CompilerParams(
            collective_id=0, has_side_effects=True, vmem_limit_bytes=64 << 20
        ),
    )(block_input, out_cotangent, weights, affine, embed, vectors, keep)
    conv_grads = conv_grads.reshape(2, 2, 3, 3, g.shard, chans)
    piece = lax.dynamic_slice_in_dim(sums, me * g.shard, g.shard, 2)
    return block_output, input_grad, conv_grads, affine_grad, piece[:, 0:2], piece[:, 2:8]


def solution(mesh):
    placed = (
        P(None, "dp", "fsdp", None, None),
        P(None, "dp", None),
        P(None, "dp", "fsdp", None, None),
        P(None, None, None, None, "fsdp", None),
        P(None, "fsdp", None),
        P(None, None, "fsdp"),
        P(None, None, "fsdp"),
        P("dp"),
    )
    return jax.shard_map(
        on_device,
        mesh=mesh,
        in_specs=placed,
        out_specs=(
            P(None, "dp", "fsdp", None, None),
            P(None, "dp", "fsdp", None, None),
            P(None, None, None, None, "fsdp", None),
            P(None, "fsdp", None),
            P(None, None, "fsdp"),
            P(None, None, "fsdp"),
        ),
        check_vma=False,
    )
```

time: 1010 us -> 248 us (0.25)
  matrix products: 517 us -> 0 us
  Pallas kernels: 0 us -> 223 us
  blocking collectives: 159 us -> 0 us
  other arithmetic: 118 us -> 1.22 us
  starting transfers between devices: 67.5 us -> 0 us
  local copies, waits for them, and re-layouts: 79.2 us -> 22.5 us
  waiting for transfers between devices: 45.6 us -> 0 us
  between operations: 17.9 us -> 1.34 us
    dot_general x149 -> x0, matrix products: 517 us -> none  [the longest x54 243 us: conv_back(): jnp.einsum('bhwd,cd->bhwc', window, kernel[row_tap, col_tap], preferred_e...]
    pallas_call x0 -> x1, Pallas kernels: none -> 223 us  [on_device(): pl.pallas_call(functools.partial(kernel_body, g), out_shape=(jax.ShapeDty...]
    psum x5 -> x0, blocking collectives: 83.6 us -> none  [the longest x1 59 us: on_device(): lax.psum((kernel_piece, gain_piece, jnp.concatenate([bias_piece, mod_piec...]
    all_gather x9 -> x0, blocking collectives: 75.2 us -> none  [the longest x3 41.4 us: on_device(): lax.all_gather(affine_weight[network], 'fsdp', axis=0, tiled=True)]
    ppermute x24 -> x0, starting transfers between devices: 66.5 us -> none  [the longest x12 50.6 us: extended(): before = lax.ppermute(last, axis, up)]
    psum x1 -> x0, waiting for transfers between devices: 44.7 us -> none  [on_device(): lax.psum((kernel_piece, gain_piece, jnp.concatenate([bias_piece, mod_piec...]
    another operation x32 -> x0, other arithmetic: 35 us -> none  [the longest x3 15.8 us: on_device(): jnp.stack(in_grads)]
    reduce_sum x30 -> x0, other arithmetic: 34.6 us -> none  [the longest x2 15.5 us: on_device(): jnp.sum(hidden_grad, axis=(0, 1, 2))]
  transfers between devices with their start and end apart: 34 -> 0, of which waited for: 1 -> 0; matrix products, arithmetic and copies ran while one was open for 41% -> 0% of each run, Pallas kernels for 0% -> 0%
where the time goes in v1:
time: 248 us
  Pallas kernels  223 us (90%)
  local copies, waits for them, and re-layouts  22.5 us (9%)
    pallas_call x1, Pallas kernels, on_device(): pl.pallas_call(functools.partial(kernel_body, g), out_shape=(jax.ShapeDty...  223 us
    unnamed x14, local copies, waits for them, and re-layouts  17.2 us

profile of v1, /device:TPU:0, one launch (start us, length us, event | category | flops | bytes accessed | tf_op | source)
XLA Modules:
  0.0 247.8 jit_solution(10948657304888257557)
XLA Ops:
  0.6 0.7 maximum_convert_fusion
  1.4 0.3 dynamic_update_slice.3.gb
  1.7 0.0 copy-start.3
  1.7 0.7 constant_dynamic-slice_fusion.2
  2.4 0.0 copy-done.3
  2.4 0.6 broadcast_in_dim.4.emb
  3.0 2.5 copy.15
  5.5 1.4 copy.16
  7.6 0.5 compare_convert_fusion.keep
  8.1 222.8 %shard_map.127 = (bf16[3,2,32,64,192]{4,3,2,1,0:T(8,128)(2,1)}, bf16[3,2,32,64,192]{4,3,2,1,0:T(8,128)(2,1)}, f32[2,2,864,192]{3,2,1,0:T(8,128)}, f32[2,384,384]{2,1,0:T(8,128)}, f32[2,8,192]{2,1,0:T(8,128)}) custom-call(bf16[3,2,32,64,192]{4,3,2,1,0:T(8,128)(2,1)} %x_h.1, bf16[3,2,32,64,192]{4,3,2,1,0:T(8,128)(2,1)} %gy_h.1, ...), custom_call_target="tpu_custom_call" | custom-call | tf_op jit(solution)/shard_map/pallas_call | solution.py:898
  230.9 0.8 constant_dynamic-slice_fusion.1
  231.7 0.6 copy.17
  232.3 1.4 constant_dynamic-slice_fusion
  233.7 0.0 copy-start
  233.7 6.8 %copy.24 = bf16[3,2,32,64,192]{4,3,2,1,0:T(8,128)(2,1)} copy(bf16[3,2,32,64,192]{4,3,2,1,0:T(8,128)(2,1)} %get-tuple-element.34) | data formatting | bytes 9437184
  240.4 0.0 copy-done
  240.4 0.0 copy-start.1
  240.4 3.2 %copy.25 = bf16[3,2,32,64,192]{4,3,2,1,0:T(8,128)(2,1)} copy(bf16[3,2,32,64,192]{4,3,2,1,0:T(8,128)(2,1)S(1)} %copy-done) | data formatting | bytes 9437184
  243.6 1.1 copy-done.1
  244.7 0.0 copy-start.2
  244.7 1.8 copy.26
  246.5 0.3 copy-done.2
  246.8 1.0 copy.27
  (1 shorter events, 0.0 us)
Async XLA Ops:
  1.7 0.7 copy-start.3
  233.7 6.8 %copy-start = (bf16[3,2,32,64,192]{4,3,2,1,0:T(8,128)(2,1)S(1)}, bf16[3,2,32,64,192]{4,3,2,1,0:T(8,128)(2,1)}, u32[]{:S(2)}) copy-start(bf16[3,2,32,64,192]{4,3,2,1,0:T(8,128)(2,1)} %get-tuple-element.35) | copy-start | bytes 14155780
  240.4 4.3 %copy-start.1 = (f32[2,2,864,192]{3,2,1,0:T(8,128)S(1)}, f32[2,2,864,192]{3,2,1,0:T(8,128)}, u32[]{:S(2)}) copy-start(f32[2,2,864,192]{3,2,1,0:T(8,128)} %get-tuple-element.13) | copy-start | bytes 7962628
  244.7 2.1 copy-start.2

commit v2 on v1

v2 whole, which is shorter than its diff:
```python
import functools
import types

import jax
import jax.numpy as jnp
from jax import lax
from jax.experimental import pallas as pl
from jax.experimental.pallas import tpu as pltpu
from jax.sharding import PartitionSpec as P

GROUPS = 32
EPSILON = 1e-05
LANES = 128
CHUNK = 64
MESH = pl.DeviceIdType.MESH
F32 = jnp.float32
BF16 = jnp.bfloat16

MU0, R0, G0, G1, B1, B2, B3, SC1, SH, SGY, MU1, R1, SUMH = range(13)
PA0, PB0, PMU0, PBIAS, PA1, PB1, PMU1, PDA, PDB, PDC = range(10)


def settings(dp_size, fsdp_size, nets, slots, rows, width, chans, embed_rows):
    g = types.SimpleNamespace()
    g.dp, g.f, g.nets, g.s, g.r, g.w, g.c, g.ef = (
        dp_size, fsdp_size, nets, slots, rows, width, chans, embed_rows,
    )
    g.np = rows // 2
    g.px = g.np * LANES
    g.count = float(rows * fsdp_size * width * (chans // GROUPS))
    g.pixels = float(rows * fsdp_size * width)
    g.bits = dp_size.bit_length() - 1
    g.shard = chans // fsdp_size
    g.low_rows = 9 * g.shard
    g.high_rows = -(-g.low_rows // 16) * 8
    g.pack = -(-(g.low_rows + g.high_rows) // 64) * 64
    g.half = g.pack // 2
    g.piece = g.pack // 8
    g.wide = max(2 * chans, embed_rows)
    g.stages = g.bits + 2
    return g


def kernel_body(
    g,
    x_h, gy_h, w_h, aff, emb, gains, biases, counts,
    y_h, dx_h, cg_h, ag_h, sg,
    rx, rg, dhp, xc, gc, xa0, xa1, xg, hb, hbuf, dub, wraw, wf, wb, gacc, pk, r0b, r1b, ry0, ry1, rbb,
    yc, ags, ex1, ex2, sb, acc, rowt, prm,
    lx, lg, ysem, hs, hr, es, er, wl, wys, wyr, wcs, wcr, cs, cr, ss, sr, osem,
):
    me = lax.axis_index("fsdp")
    dp = lax.axis_index("dp")
    C, NP, F, S, R = g.c, g.np, g.f, g.s, g.r
    PX = g.px

    def net_of(i):
        return (2 * i) % g.nets

    def peer(df):
        return (me + df) % F

    def source(df):
        return (me + F - df) % F

    def bit(b):
        return (dp // (1 << b)) % 2

    def other(*bits):
        where = dp
        for b in bits:
            where = where + (1 << b) * (1 - 2 * bit(b))
        return where

    def remote(src, dst, send, recv, where):
        return pltpu.make_async_remote_copy(
            src_ref=src, dst_ref=dst, send_sem=send, recv_sem=recv,
            device_id=where, device_id_type=MESH,
        )

    def tile(t):
        if isinstance(t, int):
            return pl.ds(t * LANES, LANES)
        return pl.ds(pl.multiple_of(t * LANES, LANES), LANES)

    def kept(s):
        return jnp.where(s < counts[0], 1.0, 0.0)

    lane = lax.broadcasted_iota(jnp.int32, (C, LANES), 1)
    low_lanes = lane < g.w
    top = (me > 0).astype(jnp.int32)
    bottom = (me < F - 1).astype(jnp.int32)
    edge_ok = jnp.where(low_lanes, top, bottom) > 0


    def halo_copy(i, s, t, down):
        src = (x_h, gy_h)[t]
        n = net_of(i)
        if down:
            return remote(
                src.at[n, s, pl.ds(R - 2, 2)], hb.at[i % 2, s, t, 0],
                hs.at[i, s, t, 1], hr.at[i, s, t, 1], {"fsdp": (me + 1) % F},
            )
        return remote(
            src.at[n, s, pl.ds(0, 2)], hb.at[i % 2, s, t, 1],
            hs.at[i, s, t, 0], hr.at[i, s, t, 0], {"fsdp": (me + F - 1) % F},
        )

    def halo_start(i, s, t):
        @pl.when(me > 0)
        def _():
            halo_copy(i, s, t, False).start()

        @pl.when(me < F - 1)
        def _():
            halo_copy(i, s, t, True).start()

    def halo_take(i, s, t):
        @pl.when(me > 0)
        def _():
            halo_copy(i, s, t, True).wait_recv()

        @pl.when(me < F - 1)
        def _():
            halo_copy(i, s, t, False).wait_recv()

    def halo_sent(i, s, t):
        @pl.when(me > 0)
        def _():
            halo_copy(i, s, t, False).wait_send()

        @pl.when(me < F - 1)
        def _():
            halo_copy(i, s, t, True).wait_send()

    def row_copy(i, e, s, df, who):
        ref = ex1.at[i, s, who] if e == 0 else ex2.at[i, e - 1, s, who]
        return remote(ref, ref, es.at[i, e, s, df], er.at[i, e, s, df], {"fsdp": peer(df)})

    def rows_start(i, e, s):
        for df in range(1, F):
            row_copy(i, e, s, df, me).start()

    def rows_take(i, e, s):
        for df in range(1, F):
            row_copy(i, e, s, df, source(df)).wait_recv()
        parts = [ex1[i, s, f] if e == 0 else ex2[i, e - 1, s, f] for f in range(F)]
        total = parts[0]
        for part in parts[1:]:
            total = total + part
        return total

    mine = dp % 2

    def weight_copy(i, df, who):
        return remote(
            w_h.at[net_of(i), mine], wraw.at[i % 2, who, mine],
            wys.at[i, df], wyr.at[i, df], {"fsdp": peer(df)},
        )

    def weight_share(i, df, kind):
        ref = wraw.at[i % 2, source(df), kind]
        return remote(ref, ref, wcs.at[i, df], wcr.at[i, df], {"dp": other(0)})

    def weight_local(i):
        return pltpu.make_async_copy(w_h.at[net_of(i)], wraw.at[i % 2, me], wl.at[i])

    def weights_start(i):
        for df in range(1, F):
            weight_copy(i, df, me).start()
        weight_local(i).start()

    def weights_forward(i):
        for df in range(1, F):
            weight_copy(i, df, source(df)).wait_recv()
            weight_share(i, df, mine).start()

    def weights_take(i):
        weight_local(i).wait()
        for df in range(1, F):
            weight_share(i, df, 1 - mine).wait_recv()

    def weights_sent(i):
        for df in range(1, F):
            weight_share(i, df, mine).wait_send()

    def halos_start(i, t):
        for s in range(S):
            halo_start(i, s, t)


    def rows_at(offset, size):
        if not isinstance(offset, int):
            offset = pl.multiple_of(offset, 8)
        return pl.ds(offset, size)

    half_start = bit(0) * g.half
    PAIR = ((1,), (2,), (1, 2))

    def piece_start(bits):
        b1 = 1 - bit(1) if 1 in bits else bit(1)
        b2 = 1 - bit(2) if 2 in bits else bit(2)
        return half_start + (2 * b1 + b2) * g.piece

    def stage_copies(m, k, t):
        def sems(j):
            return cs.at[m, k, t, j], cr.at[m, k, t, j]

        mine_at = rows_at(piece_start(()), g.piece)
        gather = g.bits
        if t == 0:
            there = rows_at((1 - bit(0)) * g.half, g.half)
            return [(remote(pk.at[m, k, :, there], r0b.at[k], *sems(0), {"dp": other(0)}), None)]
        if t in (1, 2) and (t == 1) == (k == 1):
            rows = rows_at(half_start, g.half) if k else mine_at
            into = ry1 if k else ry0
            return [
                (remote(pk.at[m, k, peer(df), rows], into.at[m, df - 1], *sems(df), {"fsdp": peer(df)}), None)
                for df in range(1, F)
            ]
        if t in (1, 2):
            copies = []
            for j, bits in enumerate(PAIR):
                rows = rows_at(piece_start(bits), g.piece)
                src = pk.at[m, k, me, rows] if k else pk.at[m, k, :, rows]
                dst = r1b.at[k, j, 0] if k else r1b.at[k, j]
                copies.append((remote(src, dst, *sems(j), {"dp": other(*bits)}), None))
            return copies
        if t < gather:
            return [(
                remote(pk.at[m, k, me, mine_at], rbb.at[k, t - 3], *sems(0), {"dp": other(t)}), None,
            )]
        if t == gather:
            own = pk.at[m, k, me, mine_at]
            return [
                (
                    remote(own, own, *sems(j), {"dp": other(*bits)}),
                    remote(own, pk.at[m, k, me, rows_at(piece_start(bits), g.piece)], *sems(j), {"dp": other(*bits)}),
                )
                for j, bits in enumerate(PAIR)
            ]
        own = pk.at[m, k, me, rows_at(half_start, g.half)]
        there = pk.at[m, k, me, rows_at((1 - bit(0)) * g.half, g.half)]
        return [(
            remote(own, own, *sems(0), {"dp": other(0)}), remote(own, there, *sems(0), {"dp": other(0)}),
        )]

    def add_rows(dst, start, sources, size):
        step = max(n for n in range(8, 65, 8) if size % n == 0)

        def body(j, carry):
            at = rows_at(start + j * step, step)
            total = dst[at, :]
            for src in sources:
                total = total + src[rows_at(j * step, step), :]
            dst[at, :] = total
            return carry

        lax.fori_loop(0, size // step, body, 0)

    def stage_start(m, k, t):
        for copy, _ in stage_copies(m, k, t):
            copy.start()

    def stage_finish(m, k, t):
        for copy, received in stage_copies(m, k, t):
            copy.wait_send()
            (received or copy).wait_recv()
        if t == 0:
            for f in range(F):
                add_rows(pk.at[m, k, f], half_start, [r0b.at[k, f]], g.half)
        elif t in (1, 2) and (t == 1) == (k == 1):
            into = ry1 if k else ry0
            start, size = (half_start, g.half) if k else (piece_start(()), g.piece)
            add_rows(pk.at[m, k, me], start, [into.at[m, df - 1] for df in range(1, F)], size)
        elif t in (1, 2):
            if k:
                add_rows(pk.at[m, k, me], piece_start(()), [r1b.at[k, j, 0] for j in range(3)], g.piece)
            else:
                for f in range(F):
                    add_rows(pk.at[m, k, f], piece_start(()), [r1b.at[k, j, f] for j in range(3)], g.piece)
        elif t < g.bits:
            add_rows(pk.at[m, k, me], piece_start(()), [rbb.at[k, t - 3]], g.piece)

    def small_copies(m, r, received):
        groups = [((0,),), PAIR]
        if r < 2:
            size, targets, sem = (1, groups[0], 0) if r == 0 else (2, groups[1], 1)
        else:
            size, targets, sem = 1 << (r + 1), ((r + 1,),), r + 2
        copies = []
        for j, bits in enumerate(targets):
            own = sb.at[m, pl.ds((dp // size) * size, size)]
            dst = sb.at[m, pl.ds((other(*bits) // size) * size, size)] if received else own
            copies.append(remote(own, dst, ss.at[m, sem + j], sr.at[m, sem + j], {"dp": other(*bits)}))
        return copies

    def small_start(m, r):
        for copy in small_copies(m, r, False):
            copy.start()

    def small_finish(m, r):
        for copy in small_copies(m, r, False):
            copy.wait_send()
        for copy in small_copies(m, r, True):
            copy.wait_recv()

    rounds = [(2, 3), (3, 4)] + [(b + 1, b + 2) for b in range(3, g.bits)]

    def tick(m, t):
        if t == 0:
            for k in range(2):
                pack_rows(m, k)
                stage_start(m, k, 0)
            return
        for k in range(2):
            stage_finish(m, k, t - 1)
        for r, (_, last) in enumerate(rounds):
            if t == last:
                small_finish(m, r)
        for r, (first, _) in enumerate(rounds):
            if t == first:
                small_start(m, r)
        if t < g.stages:
            for k in range(2):
                stage_start(m, k, t)
        else:
            for k in range(2):
                pltpu.make_async_copy(pk.at[m, k, me], cg_h.at[m, k], osem.at[m, k]).start()
        if t == rounds[-1][1]:
            finish_small(m)

    def finish_small(m):
        total = sb[m, 0, 0:8, 0 : 2 * LANES]
        for d in range(1, g.dp):
            total = total + sb[m, d, 0:8, 0 : 2 * LANES]
        sg[m] = pltpu.roll(total, 2 * LANES - me * g.shard, 1)
        block = sb[m, :, 8:16, :].reshape(g.dp * 8, g.wide)
        index = lax.broadcasted_iota(jnp.int32, (g.dp * 8, g.ef), 0) & 7
        left = jnp.where(index < S, block[:, : g.ef], 0.0).astype(BF16)
        right = pltpu.roll(block[:, : 2 * C], g.dp * 8 - S, 0).astype(BF16)
        if m > 0:
            pltpu.make_async_copy(ags, ag_h.at[m - 1], osem.at[m - 1, 2]).wait()
        ags[...] = lax.dot_general(left, right, (((0,), (0,)), ((), ())), preferred_element_type=F32)
        pltpu.make_async_copy(ags, ag_h.at[m], osem.at[m, 2]).start()

    def pack_rows(m, k):
        for f in range(F):
            for tap in range(9):
                first, last = tap * g.shard, (tap + 1) * g.shard
                c0 = tap * C + f * g.shard
                pk[m, k, f, first:last, :] = gacc[k, c0 : c0 + g.shard, 0:LANES]
                for lo, hi, lanes in ((0, g.high_rows, 0), (g.high_rows, g.low_rows, CHUNK)):
                    a, b = max(first, lo), min(last, hi)
                    if a < b:
                        at = g.low_rows + a - lo
                        pk[m, k, f, at : at + b - a, lanes : lanes + C - LANES] = gacc[
                            k, c0 + a - first : c0 + b - first, LANES:C
                        ]


    def shifted(v):
        col = lax.broadcasted_iota(jnp.int32, v.shape, 1) & (g.w - 1)
        left = jnp.where(col == 0, 0.0, pltpu.roll(v, 1, 1))
        right = jnp.where(col == g.w - 1, 0.0, pltpu.roll(v, LANES - 1, 1))
        return left, v, right

    def put(buf, s, rows, t, v):
        for j, moved in enumerate(shifted(v)):
            buf[s, j, rows, tile(t)] = moved.astype(BF16)

    def put_edges(buf, s, first_edge, second_edge):
        near = shifted(first_edge)
        far = None if second_edge is None else shifted(second_edge)
        for j in range(3):
            first = buf[s, j, :, tile(1)].astype(F32)
            last = buf[s, j, :, tile(NP)].astype(F32)
            buf[s, j, :, tile(0)] = jnp.where(low_lanes, near[j], pltpu.roll(last, g.w, 1)).astype(BF16)
            buf[s, j, :, tile(NP + 1)] = jnp.where(low_lanes, pltpu.roll(first, g.w, 1), near[j]).astype(BF16)
            if far is not None:
                buf[s, j, :, tile(NP + 2)] = jnp.where(low_lanes, far[j], last).astype(BF16)
                buf[s, j, :, tile(NP + 3)] = near[j].astype(BF16)
                buf[s, j, :, tile(NP + 4)] = jnp.where(low_lanes, first, far[j]).astype(BF16)

    def windows(buf, s, back, edge):
        pieces = []
        for i in range(3):
            for j in range(3):
                ti, tj = (2 - i, 2 - j) if back else (i, j)
                piece = buf[s, tj, :, ti * LANES : ti * LANES + PX]
                if edge:
                    piece = jnp.concatenate([piece, buf[s, tj, :, tile(NP + 2 + ti)]], axis=1)
                pieces.append(piece)
        return jnp.concatenate(pieces, axis=0)

    def chunks():
        return [pl.ds(c0, CHUNK) for c0 in range(0, C, CHUNK)]

    def quads():
        order = [NP - 1] + list(range(NP - 1))
        return [order[q : q + 4] for q in range(0, NP, 4)]

    def clear(count):
        for k in range(count):
            acc[k] = jnp.zeros((C, LANES), F32)

    def total_row(k):
        return jnp.sum(acc[k].T, axis=0, keepdims=True)

    def group_rows(rows):
        high = rows.astype(BF16)
        rest = rows - high.astype(F32)
        middle = rest.astype(BF16)
        low = (rest - middle.astype(F32)).astype(BF16)
        a = lax.broadcasted_iota(jnp.int32, (C, C), 0) // (C // GROUPS)
        b = lax.broadcasted_iota(jnp.int32, (C, C), 1) // (C // GROUPS)
        same = jnp.where(a == b, 1.0, 0.0).astype(BF16)
        three = jnp.dot(jnp.concatenate([high, middle, low], axis=0).astype(BF16), same, preferred_element_type=F32)
        n = rows.shape[0]
        return three[0:n] + three[n : 2 * n] + three[2 * n : 3 * n]

    def stack(*rows):
        fill = 8 - len(rows)
        return jnp.concatenate(list(rows) + [jnp.zeros((fill, C), F32)] * (fill > 0), axis=0)

    def spread(s, k, row):
        prm[s, k] = jnp.broadcast_to(row, (LANES, C)).T

    def save(s, k, row):
        rowt[s, k : k + 1, :] = row

    def row(s, k):
        return rowt[s, k : k + 1, :]

    def moments(total):
        grouped = group_rows(total)
        mean = grouped[0:1] / g.count
        variance = grouped[1:2] / g.count - mean * mean
        return mean, lax.rsqrt(variance + EPSILON)

    def slope_twice(w, t):
        return (1.0 + t) * (1.0 + w * (1.0 - t))

    def pair(buf, s, q):
        return jnp.concatenate([buf[s, q], buf[s, q + NP]], axis=0)

    def pixels(buf, s):
        return jnp.concatenate([buf[s, h] for q in range(NP) for h in (q, q + NP)], axis=0)

    def own_embedding(n):
        whole = emb[n].astype(F32)
        return pltpu.roll(whole, whole.shape[1] - me * g.ef, 1)[:, 0 : g.ef]


    def sums_phase(i, s):
        n = net_of(i)
        pltpu.make_async_copy(x_h.at[n, s], rx.at[s], lx.at[s]).wait()

        def step(h, carry):
            a, b = carry
            v = rx[s, h].astype(F32)
            v = v.reshape(g.w // 8, 8, C)
            return a + jnp.sum(v, axis=0), b + jnp.sum(v * v, axis=0)

        zero = jnp.zeros((8, C), F32)
        a, b = lax.fori_loop(0, R, step, (zero, zero), unroll=4)
        mod = jnp.dot(own_embedding(n).astype(BF16), aff[n], preferred_element_type=F32)
        which = lax.broadcasted_iota(jnp.int32, mod.shape, 0) == s
        mod = jnp.sum(jnp.where(which, mod, 0.0), axis=0, keepdims=True)
        ex1[i, s, me, 0:8] = stack(
            jnp.sum(a, axis=0, keepdims=True), jnp.sum(b, axis=0, keepdims=True), mod[:, 0:C], mod[:, C : 2 * C],
        )
        vectors = jnp.concatenate([gains[n], biases[n]], axis=0).astype(F32)
        vectors = jnp.concatenate([vectors, jnp.zeros((8, 2 * LANES - g.shard), F32)], axis=1)
        ex1[i, s, me, 8:16] = pltpu.roll(vectors, me * g.shard, 1)[:, 0:C]
        rows_start(i, 0, s)

    def weights_ready(i):
        for k in range(2):
            for tap in range(9):
                blocks = [wraw[i % 2, f, k, tap] for f in range(F)]
                if g.shard % 16:
                    blocks = [b.astype(F32) for b in blocks]
                whole = jnp.concatenate(blocks, axis=0).astype(BF16)
                wb[k, :, tap * C : (tap + 1) * C] = whole
                wf[k, :, tap * C : (tap + 1) * C] = whole.T

    def edge_tiles(i, s, t):
        near = jnp.concatenate([hb[i % 2, s, t, 0, 1], hb[i % 2, s, t, 1, 0]], axis=0).T.astype(F32)
        far = jnp.concatenate([hb[i % 2, s, t, 0, 0], hb[i % 2, s, t, 1, 1]], axis=0).T.astype(F32)
        return near, far

    def first_phase(i, s):
        kf = kept(s)
        pltpu.make_async_copy(gy_h.at[net_of(i), s], rg.at[s], lg.at[s]).wait()
        halo_take(i, s, 0)
        halo_take(i, s, 1)
        total = rows_take(i, 0, s)
        mean, inverse = moments(total[0:8])
        save(s, MU0, mean)
        save(s, R0, inverse)
        gain0, gain1 = total[8:9], total[9:10]
        save(s, G0, gain0)
        save(s, G1, gain1)
        save(s, B2, total[12:13])
        save(s, B3, total[13:14])
        save(s, SC1, total[2:3] + total[14:15] + 1.0)
        save(s, SH, total[3:4] + total[15:16])
        scale = inverse * gain0
        spread(s, PA0, 0.5 * scale)
        spread(s, PB0, 0.5 * (total[10:11] - mean * scale))
        spread(s, PMU0, mean)
        spread(s, PBIAS, total[11:12])
        clear(3)

        def act(xf, a, b):
            w = xf * a + b
            return w * jnp.tanh(w) + w

        def body(qs):
            for q in qs:
                xc[s, :, tile(q)] = pair(rx, s, q).T
            for rows in chunks():
                a, b = prm[s, PA0, rows], prm[s, PB0, rows]
                for q in qs:
                    put(xa0, s, rows, q + 1, act(xc[s, rows, tile(q)].astype(F32), a, b))

        def edges():
            near, far = edge_tiles(i, s, 0)
            near = jnp.where(edge_ok, act(near, prm[s, PA0], prm[s, PB0]), 0.0)
            far = jnp.where(edge_ok, act(far, prm[s, PA0], prm[s, PB0]), 0.0)
            put_edges(xa0, s, near, far)

        for n, qs in enumerate(quads()):
            body(qs)
            if n == 0:
                edges()
        hbuf[s] = jnp.dot(wf[0], windows(xa0, s, False, True), preferred_element_type=F32)
        for q in range(NP + 1):
            for rows in chunks():
                h = hbuf[s, rows, tile(q)] + prm[s, PBIAS, rows]
                hbuf[s, rows, tile(q)] = h
                if q < NP:
                    acc[0, rows] = acc[0, rows] + h
                    acc[1, rows] = acc[1, rows] + h * h
        for qs in quads():
            for q in qs:
                gc[s, :, tile(q)] = (pair(rg, s, q).T.astype(F32) * kf).astype(BF16)
            for rows in chunks():
                a2 = acc[2, rows]
                for q in qs:
                    gf = gc[s, rows, tile(q)].astype(F32)
                    a2 = a2 + gf
                    put(xg, s, rows, q + 1, gf)
                acc[2, rows] = a2
        near, far = edge_tiles(i, s, 1)
        put_edges(xg, s, jnp.where(edge_ok, near, 0.0) * kf, jnp.where(edge_ok, far, 0.0) * kf)
        ex2[i, 0, s, me] = stack(total_row(0), total_row(1), total_row(2))
        rows_start(i, 1, s)

    def second_phase(i, s):
        total = rows_take(i, 1, s)
        mean, inverse = moments(total)
        save(s, MU1, mean)
        save(s, R1, inverse)
        save(s, SUMH, total[0:1])
        save(s, SGY, total[2:3])
        scale = inverse * row(s, G1)
        spread(s, PA1, 0.5 * scale * row(s, SC1))
        spread(s, PB1, 0.5 * (row(s, SH) + (row(s, B2) - mean * scale) * row(s, SC1)))
        spread(s, PMU1, mean)
        clear(2)
        dub[s] = jnp.dot(wb[1], windows(xg, s, True, True), preferred_element_type=F32)
        for q in range(NP + 1):
            for rows in chunks():
                a, b, mu = prm[s, PA1, rows], prm[s, PB1, rows], prm[s, PMU1, rows]
                h = hbuf[s, rows, tile(q)]
                w = h * a + b
                t = jnp.tanh(w)
                d = dub[s, rows, tile(q)] * slope_twice(w, t)
                dub[s, rows, tile(q)] = d
                if q < NP:
                    put(xa1, s, rows, q + 1, w * t + w)
                    acc[0, rows] = acc[0, rows] + d
                    acc[1, rows] = acc[1, rows] + d * (h - mu)
        w = hbuf[s, :, tile(NP)] * prm[s, PA1] + prm[s, PB1]
        put_edges(xa1, s, jnp.where(edge_ok, w * jnp.tanh(w) + w, 0.0), None)
        ex2[i, 1, s, me] = stack(0.5 * total_row(0), 0.5 * total_row(1))
        rows_start(i, 2, s)

    def out_copy(i, s):
        return pltpu.make_async_copy(yc.at[s], y_h.at[net_of(i), s], ysem.at[s])

    def in_grad_copy(i, s):
        return pltpu.make_async_copy(yc.at[s], dx_h.at[net_of(i), s], ysem.at[s])

    def third_phase(i, s):
        kf = kept(s)

        @pl.when(i > 0)
        def _():
            in_grad_copy(i, s).wait()

        total = rows_take(i, 2, s)
        s1, s2 = total[0:1], total[1:2] * row(s, R1)
        sc1, gain1, inverse, mean = row(s, SC1), row(s, G1), row(s, R1), row(s, MU1)
        grouped = group_rows(stack(gain1 * sc1 * s1, gain1 * sc1 * s2))
        m1, m2 = grouped[0:1] / g.count, grouped[1:2] / g.count
        a = inverse * sc1 * gain1
        b = -inverse * inverse * m2
        c = -inverse * m1 - mean * b
        spread(s, PDA, 0.5 * a)
        spread(s, PDB, b)
        spread(s, PDC, c)
        spread(s, PBIAS, row(s, B3))
        dscale = gain1 * s2 + row(s, B2) * s1
        here = sb.at[i, dp]
        here[1:2, 0:C] = here[1:2, 0:C] + sc1 * s2
        here[3:4, 0:C] = here[3:4, 0:C] + a * s1 + b * row(s, SUMH) + c * g.pixels
        here[4:5, 0:C] = here[4:5, 0:C] + sc1 * s1
        here[5:6, 0:C] = here[5:6, 0:C] + row(s, SGY)
        here[6:7, 0:C] = here[6:7, 0:C] + dscale
        here[7:8, 0:C] = here[7:8, 0:C] + s1
        modulation = jnp.concatenate([dscale, s1], axis=1).astype(BF16).astype(F32)
        for slot in range(S):
            at = 8 + S + slot
            here[at : at + 1, 0 : 2 * C] = jnp.where(s == slot, modulation, here[at : at + 1, 0 : 2 * C])

        def hidden_grad(with_weights):
            for n, qs in enumerate(quads()):
                for rows in chunks():
                    pa, pb, pc = prm[s, PDA, rows], prm[s, PDB, rows], prm[s, PDC, rows]
                    for q in qs:
                        d = dub[s, rows, tile(q)] * pa + hbuf[s, rows, tile(q)] * pb + pc
                        put(xg, s, rows, q + 1, d)
                if with_weights:
                    for q in qs:
                        flat = xg[s, 1, :, tile(q + 1)].T
                        dhp[s, q] = flat[0 : g.w]
                        dhp[s, q + NP] = flat[g.w : 2 * g.w]
                if n == 0:
                    d = dub[s, :, tile(NP)] * prm[s, PDA] + hbuf[s, :, tile(NP)] * prm[s, PDB] + prm[s, PDC]
                    put_edges(xg, s, jnp.where(edge_ok, d, 0.0), None)
            if with_weights:
                o = jnp.dot(windows(xa1, s, False, False), pixels(rg, s), preferred_element_type=F32)
                gacc[1] = gacc[1] + o * kf

        def output(with_weights):
            dub[s, :, 0:PX] = jnp.dot(wf[1], windows(xa1, s, False, False), preferred_element_type=F32)
            for q in range(NP):
                for rows in chunks():
                    v = dub[s, rows, tile(q)] + prm[s, PBIAS, rows]
                    v = (v + xc[s, rows, tile(q)].astype(F32)) * kf
                    yc[s, rows, tile(q)] = v.astype(BF16)
            if with_weights:
                gacc[0] = gacc[0] + jnp.dot(windows(xa0, s, False, False), pixels(dhp, s), preferred_element_type=F32)

        for piece in (hidden_grad, output):
            pl.when(i < 2)(functools.partial(piece, True))
            pl.when(i == 2)(functools.partial(piece, False))

        out_copy(i, s).start()

    def fourth_phase(i, s):
        clear(2)
        hbuf[s, :, 0:PX] = jnp.dot(wb[0], windows(xg, s, True, False), preferred_element_type=F32)
        for q in range(NP):
            for rows in chunks():
                xf = xc[s, rows, tile(q)].astype(F32)
                w = xf * prm[s, PA0, rows] + prm[s, PB0, rows]
                d = hbuf[s, rows, tile(q)] * slope_twice(w, jnp.tanh(w))
                hbuf[s, rows, tile(q)] = d
                acc[0, rows] = acc[0, rows] + d
                acc[1, rows] = acc[1, rows] + d * (xf - prm[s, PMU0, rows])
        ex2[i, 2, s, me] = stack(0.5 * total_row(0), 0.5 * total_row(1))
        rows_start(i, 3, s)

    def last_phase(i, s):
        total = rows_take(i, 3, s)
        inverse, mean, gain0 = row(s, R0), row(s, MU0), row(s, G0)
        s3, s4 = total[0:1], total[1:2] * inverse
        grouped = group_rows(stack(gain0 * s3, gain0 * s4))
        m1, m2 = grouped[0:1] / g.count, grouped[1:2] / g.count
        b = -inverse * inverse * m2
        spread(s, PA1, 0.5 * inverse * gain0)
        spread(s, PB1, b)
        spread(s, PMU1, -inverse * m1 - mean * b)
        here = sb.at[i, dp]
        here[0:1, 0:C] = here[0:1, 0:C] + s4
        here[2:3, 0:C] = here[2:3, 0:C] + s3
        out_copy(i, s).wait()
        for qs in quads():
            for rows in chunks():
                pa, pb, pc = prm[s, PA1, rows], prm[s, PB1, rows], prm[s, PMU1, rows]
                for q in qs:
                    xf = xc[s, rows, tile(q)].astype(F32)
                    v = hbuf[s, rows, tile(q)] * pa + xf * pb + pc + gc[s, rows, tile(q)].astype(F32)
                    yc[s, rows, tile(q)] = v.astype(BF16)
        in_grad_copy(i, s).start()


    final = list(range(5, g.stages + 1))
    plan = {
        (0, 3, S - 1): [(0, 0)],
        (0, 4, S - 1): [(0, 1)],
        (1, 2, 0): [(0, 2)],
        (1, 3, 0): [(0, 3)],
        (1, 3, S - 1): [(1, 0)],
        (1, 4, S - 1): [(0, 4), (1, 1)],
        (2, 1, S - 1): [(0, t) for t in final[:-1]],
        (2, 2, 0): [(1, 2)],
        (2, 2, S - 1): [(0, final[-1])],
        (2, 3, 0): [(1, 3)],
        (2, 5, S - 1): [(1, 4)] + [(1, t) for t in final],
    }

    def slots(number, phase, i):
        def step(s, carry):
            phase(i, s)
            for (at, where, slot), ticks in plan.items():
                if where == number:
                    @pl.when((i == at) & (s == slot))
                    def _():
                        for m, t in ticks:
                            tick(m, t)
            return carry

        lax.fori_loop(0, S, step, 0)

    def load_x(i):
        for s in range(S):
            pltpu.make_async_copy(x_h.at[net_of(i), s], rx.at[s], lx.at[s]).start()

    def load_gy(i):
        for s in range(S):
            pltpu.make_async_copy(gy_h.at[net_of(i), s], rg.at[s], lg.at[s]).start()

    load_x(0)
    load_gy(0)
    fill = g.low_rows + g.high_rows
    pk[:, :, :, fill:, :] = jnp.zeros((2, 2, F, g.pack - fill, LANES), F32)
    sb[:, dp] = jnp.zeros((3, 16, g.wide), F32)
    for n in range(g.nets):
        own = own_embedding(n)
        for i in range(3):
            if (2 * i) % g.nets == n:
                sb[i, dp, 8 : 8 + S, 0 : g.ef] = own.astype(F32)

    @pl.when(me == 0)
    def _():
        hb[:, :, :, 0] = jnp.zeros(hb.shape[:3] + hb.shape[4:], BF16)

    @pl.when(me == F - 1)
    def _():
        hb[:, :, :, 1] = jnp.zeros(hb.shape[:3] + hb.shape[4:], BF16)

    barrier = pltpu.get_barrier_semaphore()
    partners = [(b,) for b in range(g.bits)] + [(1, 2)]
    for df in range(1, F):
        pl.semaphore_signal(barrier, inc=1, device_id={"fsdp": peer(df)}, device_id_type=MESH)
    for bits in partners:
        pl.semaphore_signal(barrier, inc=1, device_id={"dp": other(*bits)}, device_id_type=MESH)
    pl.semaphore_wait(barrier, F - 1 + len(partners))
    halos_start(0, 0)
    weights_start(0)
    slots(0, sums_phase, 0)
    halos_start(0, 1)

    def network(i, carry):
        @pl.when(i < 2)
        def _():
            gacc[...] = jnp.zeros(gacc.shape, F32)

        weights_forward(i)
        weights_take(i)
        weights_ready(i)
        slots(1, first_phase, i)
        weights_sent(i)

        @pl.when(i < 2)
        def _():
            load_x(i + 1)
            halos_start(i + 1, 0)
            weights_start(i + 1)
            halos_start(i + 1, 1)

        slots(2, second_phase, i)
        slots(3, third_phase, i)

        @pl.when(i < 2)
        def _():
            load_gy(i + 1)

        slots(4, fourth_phase, i)

        @pl.when(i < 2)
        def _():
            slots(0, sums_phase, i + 1)

        slots(5, last_phase, i)
        return carry

    lax.fori_loop(0, 3, network, 0)


    def drain(i, carry):
        for s in range(S):
            for t in range(2):
                halo_sent(i, s, t)
            for e in range(4):
                for df in range(1, F):
                    row_copy(i, e, s, df, me).wait_send()
        for df in range(1, F):
            weight_copy(i, df, me).wait_send()
        return carry

    lax.fori_loop(0, 3, drain, 0)
    for s in range(S):
        in_grad_copy(2, s).wait()
    for m in range(2):
        for k in range(2):
            pltpu.make_async_copy(pk.at[m, k, me], cg_h.at[m, k], osem.at[m, k]).wait()
    pltpu.make_async_copy(ags, ag_h.at[1], osem.at[1, 2]).wait()


def place_body(g, y_c, dx_c, packed, affine, sums, y, dx, conv, affine_out, gain_out, bias_out):
    for src, dst in ((y_c, y), (dx_c, dx)):
        for q in range(g.np):
            flat = src[0, 0, :, q * LANES : (q + 1) * LANES].T
            dst[0, 0, q] = flat[0 : g.w]
            dst[0, 0, q + g.np] = flat[g.w : 2 * g.w]
    step = pl.program_id(0)

    @pl.when(step < 4)
    def _():
        split = g.low_rows - g.high_rows
        rest = g.c - LANES
        conv[0, 0, :, 0:LANES] = packed[0, 0, 0 : g.low_rows, :]
        conv[0, 0, 0 : g.high_rows, LANES : g.c] = packed[0, 0, g.low_rows : g.low_rows + g.high_rows, 0:rest]
        conv[0, 0, g.high_rows : g.low_rows, LANES : g.c] = packed[
            0, 0, g.low_rows : g.low_rows + split, CHUNK : CHUNK + rest
        ]

    @pl.when(step < 2)
    def _():
        affine_out[...] = affine[...]

    @pl.when(step == 0)
    def _():
        gain_out[...] = sums[:, 0:2, 0 : g.shard]
        bias_out[...] = sums[:, 2:8, 0 : g.shard]


def on_device(
    block_input, embedding, out_cotangent, conv_weights, affine_weight, gains, biases, counts
):
    nets, slots, rows, width, chans = block_input.shape
    fsdp = lax.axis_size("fsdp")
    dp = lax.axis_size("dp")
    embed_rows = affine_weight.shape[1]
    g = settings(dp, fsdp, nets, slots, rows, width, chans, embed_rows)
    weights = conv_weights.reshape(nets, 2, 9, g.shard, chans)

    tiles = (g.np + 1) * LANES
    dma = pltpu.SemaphoreType.DMA
    scratch = [
        pltpu.VMEM((slots, rows, width, chans), BF16),
        pltpu.VMEM((slots, rows, width, chans), BF16),
        pltpu.VMEM((slots, rows, width, chans), BF16),
        pltpu.VMEM((slots, chans, g.px), BF16),
        pltpu.VMEM((slots, chans, g.px), BF16),
        pltpu.VMEM((slots, 3, chans, (g.np + 5) * LANES), BF16),
        pltpu.VMEM((slots, 3, chans, (g.np + 2) * LANES), BF16),
        pltpu.VMEM((slots, 3, chans, (g.np + 5) * LANES), BF16),
        pltpu.VMEM((2, slots, 2, 2, 2, width, chans), BF16),
        pltpu.VMEM((slots, chans, tiles), F32),
        pltpu.VMEM((slots, chans, tiles), F32),
        pltpu.VMEM((2, fsdp, 2, 9, g.shard, chans), BF16),
        pltpu.VMEM((2, chans, 9 * chans), BF16),
        pltpu.VMEM((2, chans, 9 * chans), BF16),
        pltpu.VMEM((2, 9 * chans, chans), F32),
        pltpu.VMEM((2, 2, fsdp, g.pack, LANES), F32),
        pltpu.VMEM((2, fsdp, g.half, LANES), F32),
        pltpu.VMEM((2, 3, fsdp, g.piece, LANES), F32),
        pltpu.VMEM((2, fsdp - 1, g.piece, LANES), F32),
        pltpu.VMEM((2, fsdp - 1, g.half, LANES), F32),
        pltpu.VMEM((2, g.bits - 3, g.piece, LANES), F32),
        pltpu.VMEM((slots, chans, g.px), BF16),
        pltpu.VMEM((embed_rows, 2 * chans), F32),
        pltpu.VMEM((3, slots, fsdp, 16, chans), F32),
        pltpu.VMEM((3, 3, slots, fsdp, 8, chans), F32),
        pltpu.VMEM((3, dp, 16, g.wide), F32),
        pltpu.VMEM((3, chans, LANES), F32),
        pltpu.VMEM((slots, 16, chans), F32),
        pltpu.VMEM((slots, 10, chans, LANES), F32),
        dma((slots,)),
        dma((slots,)),
        dma((slots,)),
        dma((3, slots, 2, 2)),
        dma((3, slots, 2, 2)),
        dma((3, 4, slots, fsdp)),
        dma((3, 4, slots, fsdp)),
        dma((3,)),
        dma((3, fsdp)),
        dma((3, fsdp)),
        dma((3, fsdp)),
        dma((3, fsdp)),
        dma((2, 2, g.stages, max(3, fsdp))),
        dma((2, 2, g.stages, max(3, fsdp))),
        dma((2, g.bits + 2)),
        dma((2, g.bits + 2)),
        dma((2, 3)),
    ]
    hbm = pl.BlockSpec(memory_space=pl.ANY)
    vmem = pl.BlockSpec(memory_space=pltpu.VMEM)
    smem = pl.BlockSpec(memory_space=pltpu.SMEM)
    channel_major = jax.ShapeDtypeStruct((nets, slots, chans, g.px), BF16)
    main = pl.pallas_call(
        functools.partial(kernel_body, g),
        out_shape=(
            channel_major,
            channel_major,
            jax.ShapeDtypeStruct((2, 2, g.pack, LANES), F32),
            jax.ShapeDtypeStruct((2, embed_rows, 2 * chans), F32),
            jax.ShapeDtypeStruct((2, 8, 2 * LANES), F32),
        ),
        in_specs=[hbm, hbm, hbm, vmem, vmem, vmem, vmem, smem],
        out_specs=(hbm, hbm, hbm, hbm, vmem),
        scratch_shapes=scratch,
        compiler_params=pltpu.CompilerParams(
            collective_id=0, has_side_effects=True, vmem_limit_bytes=64 << 20
        ),
    )(block_input, out_cotangent, weights, affine_weight, embedding, gains, biases, counts)

    def by_slot(step):
        return (step // slots, step % slots, 0, 0)

    def by_conv(step):
        return (jnp.minimum(step, 3) // 2, jnp.minimum(step, 3) % 2, 0, 0)

    def by_net(step):
        return (jnp.minimum(step, 1), 0, 0)

    image = pl.BlockSpec((1, 1, rows, width, chans), lambda step: by_slot(step) + (0,))
    block_output, input_grad, conv_grads, affine_grad, gain_grads, bias_grads = pl.pallas_call(
        functools.partial(place_body, g),
        grid=(nets * slots,),
        out_shape=(
            jax.ShapeDtypeStruct(block_input.shape, BF16),
            jax.ShapeDtypeStruct(block_input.shape, BF16),
            jax.ShapeDtypeStruct((2, 2, g.low_rows, chans), F32),
            jax.ShapeDtypeStruct((2, embed_rows, 2 * chans), F32),
            jax.ShapeDtypeStruct((2, 2, g.shard), F32),
            jax.ShapeDtypeStruct((2, 6, g.shard), F32),
        ),
        in_specs=[
            pl.BlockSpec((1, 1, chans, g.px), by_slot),
            pl.BlockSpec((1, 1, chans, g.px), by_slot),
            pl.BlockSpec((1, 1, g.pack, LANES), by_conv),
            pl.BlockSpec((1, embed_rows, 2 * chans), by_net),
            vmem,
        ],
        out_specs=(
            image,
            image,
            pl.BlockSpec((1, 1, g.low_rows, chans), by_conv),
            pl.BlockSpec((1, embed_rows, 2 * chans), by_net),
            vmem,
            vmem,
        ),
        compiler_params=pltpu.CompilerParams(vmem_limit_bytes=48 << 20),
    )(*main)
    conv_grads = conv_grads.reshape(2, 2, 3, 3, g.shard, chans)
    return block_output, input_grad, conv_grads, affine_grad, gain_grads, bias_grads


def solution(mesh):
    placed = (
        P(None, "dp", "fsdp", None, None),
        P(None, "dp", None),
        P(None, "dp", "fsdp", None, None),
        P(None, None, None, None, "fsdp", None),
        P(None, "fsdp", None),
        P(None, None, "fsdp"),
        P(None, None, "fsdp"),
        P("dp"),
    )
    return jax.shard_map(
        on_device,
        mesh=mesh,
        in_specs=placed,
        out_specs=(
            P(None, "dp", "fsdp", None, None),
            P(None, "dp", "fsdp", None, None),
            P(None, None, None, None, "fsdp", None),
            P(None, "fsdp", None),
            P(None, None, "fsdp"),
            P(None, None, "fsdp"),
        ),
        check_vma=False,
    )
```

time: 248 us -> 183 us (0.74)
  Pallas kernels: 223 us -> 177 us
  local copies, waits for them, and re-layouts: 22.5 us -> 4.35 us
    pallas_call x1 -> x2, Pallas kernels: 223 us -> 177 us  [the longest x1 166 us: on_device(): pl.pallas_call(functools.partial(kernel_body, g), out_shape=(channel_majo...]
    unnamed x14 -> x7, local copies, waits for them, and re-layouts: 17.2 us -> 4.35 us
where the time goes in v2:
time: 183 us
  Pallas kernels  177 us (97%)
  local copies, waits for them, and re-layouts  4.35 us (2%)
    pallas_call x1, Pallas kernels, on_device(): pl.pallas_call(functools.partial(kernel_body, g), out_shape=(channel_majo...  166 us
    pallas_call x1, Pallas kernels, on_device(): pl.pallas_call(functools.partial(place_body, g), grid=(nets * slots,), ou...  11.8 us
    unnamed x7, local copies, waits for them, and re-layouts  4.35 us

profile of v2, /device:TPU:0, one launch (start us, length us, event | category | flops | bytes accessed | tf_op | source)
XLA Modules:
  0.0 183.0 jit_solution(15078252532776646802)
XLA Ops:
  1.3 165.5 %shard_map.127 = (bf16[3,2,192,2048]{3,2,1,0:T(8,128)(2,1)}, bf16[3,2,192,2048]{3,2,1,0:T(8,128)(2,1)}, f32[2,2,1344,128]{3,2,1,0:T(8,128)}, f32[2,384,384]{2,1,0:T(8,128)}, f32[2,8,256]{2,1,0:T(8,128)}) custom-call(bf16[3,2,32,64,192]{4,3,2,1,0:T(8,128)(2,1)} %x_h.1, bf16[3,2,32,64,192]{4,3,2,1,0:T(8,128)(2,1)} %gy_h.1, ...), custom_call_target="tpu_custom_call" | custom-call | tf_op jit(solution)/shard_map/pallas_call | solution.py:918
  166.8 0.0 copy-start
  166.8 1.8 copy-done
  168.6 0.0 copy-start.1
  168.6 1.3 copy-done.1
  169.9 0.0 copy-start.2
  169.9 0.7 copy-done.2
  170.6 11.8 %shard_map.128 = (bf16[3,2,32,64,192]{4,3,2,1,0:T(8,128)(2,1)}, bf16[3,2,32,64,192]{4,3,2,1,0:T(8,128)(2,1)}, f32[2,2,864,192]{3,2,1,0:T(8,128)}, f32[2,384,384]...) custom-call(bf16[3,2,192,2048]{3,2,1,0:T(8,128)(2,1)} %get-tuple-element.17.y_c, ...), custom_call_target="tpu_custom_call" | custom-call | tf_op jit(solution)/shard_map/pallas_call | solution.py:945
  182.4 0.6 copy.14
Async XLA Ops:
  166.8 1.8 copy-start
  168.6 1.3 copy-start.1
  169.9 0.7 copy-start.2

commit v3 on v2

--- a/solution.py
+++ b/solution.py
@@ -38,6 +38,8 @@
     g.piece = g.pack // 8
     g.wide = max(2 * chans, embed_rows)
     g.stages = g.bits + 2
+    g.split = 2 if g.shard % 32 == 0 else 1
+    g.rows = g.shard // g.split
     return g
 
 
@@ -45,8 +47,8 @@
     g,
     x_h, gy_h, w_h, aff, emb, gains, biases, counts,
     y_h, dx_h, cg_h, ag_h, sg,
-    rx, rg, dhp, xc, gc, xa0, xa1, xg, hb, hbuf, dub, wraw, wf, wb, gacc, pk, r0b, r1b, ry0, ry1, rbb,
-    yc, ags, ex1, ex2, sb, acc, rowt, prm,
+    rx, rg, dhp, xc, gc, xa0, xa1, xg, hb, hbuf, dub, wraw, wf, wb, gacc, pk, r0b, r1b, ryb, rbb,
+    ybuf, yc, ags, ex1, ex2, sb, acc, rowt, prm,
     lx, lg, ysem, hs, hr, es, er, wl, wys, wyr, wcs, wcr, cs, cr, ss, sr, osem,
 ):
     me = lax.axis_index("fsdp")
@@ -152,41 +154,48 @@
 
     mine = dp % 2
 
-    def weight_copy(i, df, who):
+    TRIPLES = 3
+
+    def weight_rows(half):
+        return pl.ds(pl.multiple_of(half * g.rows, g.rows), g.rows)
+
+    def weight_copy(i, k, j, df, who):
+        taps, rows = pl.ds(3 * j, 3), weight_rows(mine if g.split == 2 else 0)
         return remote(
-            w_h.at[net_of(i), mine], wraw.at[i % 2, who, mine],
-            wys.at[i, df], wyr.at[i, df], {"fsdp": peer(df)},
+            w_h.at[net_of(i), k, taps, rows], wraw.at[i % 2, who, k, taps, rows],
+            wys.at[i, k, j, df], wyr.at[i, k, j, df], {"fsdp": peer(df)},
         )
 
-    def weight_share(i, df, kind):
-        ref = wraw.at[i % 2, source(df), kind]
-        return remote(ref, ref, wcs.at[i, df], wcr.at[i, df], {"dp": other(0)})
+    def weight_share(i, k, df, half):
+        ref = wraw.at[i % 2, source(df), k, :, weight_rows(half)]
+        return remote(ref, ref, wcs.at[i, k, df], wcr.at[i, k, df], {"dp": other(0)})
 
     def weight_local(i):
         return pltpu.make_async_copy(w_h.at[net_of(i)], wraw.at[i % 2, me], wl.at[i])
 
-    def weights_start(i):
+    def weights_start(i, k, j):
         for df in range(1, F):
-            weight_copy(i, df, me).start()
-        weight_local(i).start()
-
-    def weights_forward(i):
+            weight_copy(i, k, j, df, me).start()
+
+    def weights_forward(i, k):
         for df in range(1, F):
-            weight_copy(i, df, source(df)).wait_recv()
-            weight_share(i, df, mine).start()
-
-    def weights_take(i):
-        weight_local(i).wait()
-        for df in range(1, F):
-            weight_share(i, df, 1 - mine).wait_recv()
+            for j in range(TRIPLES):
+                weight_copy(i, k, j, df, source(df)).wait_recv()
+            if g.split == 2:
+                weight_share(i, k, df, mine).start()
+
+    def weights_take(i, k):
+        if g.split == 2:
+            for df in range(1, F):
+                weight_share(i, k, df, 1 - mine).wait_recv()
 
     def weights_sent(i):
-        for df in range(1, F):
-            weight_share(i, df, mine).wait_send()
-
-    def halos_start(i, t):
-        for s in range(S):
-            halo_start(i, s, t)
+        for k in range(2):
+            for df in range(1, F):
+                for j in range(TRIPLES):
+                    weight_copy(i, k, j, df, me).wait_send()
+                if g.split == 2:
+                    weight_share(i, k, df, mine).wait_send()
 
 
     def rows_at(offset, size):
@@ -202,36 +211,37 @@
         b2 = 1 - bit(2) if 2 in bits else bit(2)
         return half_start + (2 * b1 + b2) * g.piece
 
+    def core_sums(m, k):
+        return r0b.at[0 if g.split == 2 else m, k]
+
     def stage_copies(m, k, t):
         def sems(j):
             return cs.at[m, k, t, j], cr.at[m, k, t, j]
 
         mine_at = rows_at(piece_start(()), g.piece)
-        gather = g.bits
+        own = pk.at[m, k, me, mine_at]
         if t == 0:
             there = rows_at((1 - bit(0)) * g.half, g.half)
-            return [(remote(pk.at[m, k, :, there], r0b.at[k], *sems(0), {"dp": other(0)}), None)]
-        if t in (1, 2) and (t == 1) == (k == 1):
-            rows = rows_at(half_start, g.half) if k else mine_at
-            into = ry1 if k else ry0
+            return [(remote(pk.at[m, k, :, there], core_sums(m, k), *sems(0), {"dp": other(0)}), None)]
+        if t == 1:
             return [
-                (remote(pk.at[m, k, peer(df), rows], into.at[m, df - 1], *sems(df), {"fsdp": peer(df)}), None)
+                (
+                    remote(
+                        pk.at[m, k, :, rows_at(piece_start(bits), g.piece)], r1b.at[k, j],
+                        *sems(j), {"dp": other(*bits)},
+                    ),
+                    None,
+                )
+                for j, bits in enumerate(PAIR)
+            ]
+        if t == 2:
+            return [
+                (remote(pk.at[m, k, peer(df), mine_at], ryb.at[m, k, df - 1], *sems(df - 1), {"fsdp": peer(df)}), None)
                 for df in range(1, F)
             ]
-        if t in (1, 2):
-            copies = []
-            for j, bits in enumerate(PAIR):
-                rows = rows_at(piece_start(bits), g.piece)
-                src = pk.at[m, k, me, rows] if k else pk.at[m, k, :, rows]
-                dst = r1b.at[k, j, 0] if k else r1b.at[k, j]
-                copies.append((remote(src, dst, *sems(j), {"dp": other(*bits)}), None))
-            return copies
-        if t < gather:
-            return [(
-                remote(pk.at[m, k, me, mine_at], rbb.at[k, t - 3], *sems(0), {"dp": other(t)}), None,
-            )]
-        if t == gather:
-            own = pk.at[m, k, me, mine_at]
+        if t < g.bits:
+            return [(remote(own, rbb.at[k, t - 3], *sems(0), {"dp": other(t)}), None)]
+        if t == g.bits:
             return [
                 (
                     remote(own, own, *sems(j), {"dp": other(*bits)}),
@@ -268,31 +278,30 @@
             (received or copy).wait_recv()
         if t == 0:
             for f in range(F):
-                add_rows(pk.at[m, k, f], half_start, [r0b.at[k, f]], g.half)
-        elif t in (1, 2) and (t == 1) == (k == 1):
-            into = ry1 if k else ry0
-            start, size = (half_start, g.half) if k else (piece_start(()), g.piece)
-            add_rows(pk.at[m, k, me], start, [into.at[m, df - 1] for df in range(1, F)], size)
-        elif t in (1, 2):
-            if k:
-                add_rows(pk.at[m, k, me], piece_start(()), [r1b.at[k, j, 0] for j in range(3)], g.piece)
-            else:
-                for f in range(F):
-                    add_rows(pk.at[m, k, f], piece_start(()), [r1b.at[k, j, f] for j in range(3)], g.piece)
+                add_rows(pk.at[m, k, f], half_start, [core_sums(m, k).at[f]], g.half)
+        elif t == 1:
+            for f in range(F):
+                add_rows(pk.at[m, k, f], piece_start(()), [r1b.at[k, j, f] for j in range(3)], g.piece)
+        elif t == 2:
+            add_rows(pk.at[m, k, me], piece_start(()), [ryb.at[m, k, df - 1] for df in range(1, F)], g.piece)
         elif t < g.bits:
             add_rows(pk.at[m, k, me], piece_start(()), [rbb.at[k, t - 3]], g.piece)
 
+    place = bit(1) + 2 * bit(2) + 4 * bit(0) + (dp // 8) * 8
+
     def small_copies(m, r, received):
-        groups = [((0,),), PAIR]
-        if r < 2:
-            size, targets, sem = (1, groups[0], 0) if r == 0 else (2, groups[1], 1)
-        else:
-            size, targets, sem = 1 << (r + 1), ((r + 1,),), r + 2
+        targets = PAIR if r == 0 else ((0,),) if r == 1 else ((r + 1,),)
+        size = 1 if r == 0 else 1 << (r + 1)
+        flips = {1: 1, 2: 2, 0: 4}
         copies = []
         for j, bits in enumerate(targets):
-            own = sb.at[m, pl.ds((dp // size) * size, size)]
-            dst = sb.at[m, pl.ds((other(*bits) // size) * size, size)] if received else own
-            copies.append(remote(own, dst, ss.at[m, sem + j], sr.at[m, sem + j], {"dp": other(*bits)}))
+            there = place
+            for b in bits:
+                there = there + flips.get(b, 1 << b) * (1 - 2 * bit(b))
+            own = sb.at[m, pl.ds((place // size) * size, size)]
+            dst = sb.at[m, pl.ds((there // size) * size, size)] if received else own
+            sem = j if r == 0 else r + 2
+            copies.append(remote(own, dst, ss.at[m, sem], sr.at[m, sem], {"dp": other(*bits)}))
         return copies
 
     def small_start(m, r):
@@ -304,31 +313,18 @@
             copy.wait_send()
         for copy in small_copies(m, r, True):
             copy.wait_recv()
-
-    rounds = [(2, 3), (3, 4)] + [(b + 1, b + 2) for b in range(3, g.bits)]
-
-    def tick(m, t):
+        if r == g.bits - 2:
+            finish_small(m)
+
+    def tick(m, k, t):
         if t == 0:
-            for k in range(2):
-                pack_rows(m, k)
-                stage_start(m, k, 0)
-            return
-        for k in range(2):
+            pack_rows(m, k)
+        else:
             stage_finish(m, k, t - 1)
-        for r, (_, last) in enumerate(rounds):
-            if t == last:
-                small_finish(m, r)
-        for r, (first, _) in enumerate(rounds):
-            if t == first:
-                small_start(m, r)
         if t < g.stages:
-            for k in range(2):
-                stage_start(m, k, t)
+            stage_start(m, k, t)
         else:
-            for k in range(2):
-                pltpu.make_async_copy(pk.at[m, k, me], cg_h.at[m, k], osem.at[m, k]).start()
-        if t == rounds[-1][1]:
-            finish_small(m)
+            pltpu.make_async_copy(pk.at[m, k, me], cg_h.at[m, k], osem.at[m, k]).start()
 
     def finish_small(m):
         total = sb[m, 0, 0:8, 0 : 2 * LANES]
@@ -451,6 +447,16 @@
         whole = emb[n].astype(F32)
         return pltpu.roll(whole, whole.shape[1] - me * g.ef, 1)[:, 0 : g.ef]
 
+    def weight_sums(k, acts, grads, s, factor):
+        right = pixels(grads, s)
+        for i in range(3):
+            left = jnp.concatenate(
+                [acts[s, j, :, i * LANES : i * LANES + PX] for j in range(3)], axis=0
+            )
+            rows = pl.ds(3 * C * i, 3 * C)
+            o = jnp.dot(left, right, preferred_element_type=F32)
+            gacc[k, rows] = gacc[k, rows] + (o if factor is None else o * factor)
+
 
     def sums_phase(i, s):
         n = net_of(i)
@@ -475,15 +481,14 @@
         ex1[i, s, me, 8:16] = pltpu.roll(vectors, me * g.shard, 1)[:, 0:C]
         rows_start(i, 0, s)
 
-    def weights_ready(i):
-        for k in range(2):
-            for tap in range(9):
-                blocks = [wraw[i % 2, f, k, tap] for f in range(F)]
-                if g.shard % 16:
-                    blocks = [b.astype(F32) for b in blocks]
-                whole = jnp.concatenate(blocks, axis=0).astype(BF16)
-                wb[k, :, tap * C : (tap + 1) * C] = whole
-                wf[k, :, tap * C : (tap + 1) * C] = whole.T
+    def weights_ready(i, k):
+        for tap in range(9):
+            blocks = [wraw[i % 2, f, k, tap] for f in range(F)]
+            if g.shard % 16:
+                blocks = [b.astype(F32) for b in blocks]
+            whole = jnp.concatenate(blocks, axis=0).astype(BF16)
+            wb[k, :, tap * C : (tap + 1) * C] = whole
+            wf[k, :, tap * C : (tap + 1) * C] = whole.T
 
     def edge_tiles(i, s, t):
         near = jnp.concatenate([hb[i % 2, s, t, 0, 1], hb[i % 2, s, t, 1, 0]], axis=0).T.astype(F32)
@@ -560,6 +565,7 @@
 
     def second_phase(i, s):
         total = rows_take(i, 1, s)
+        window(2, i, s)
         mean, inverse = moments(total)
         save(s, MU1, mean)
         save(s, R1, inverse)
@@ -588,6 +594,10 @@
         ex2[i, 1, s, me] = stack(0.5 * total_row(0), 0.5 * total_row(1))
         rows_start(i, 2, s)
 
+        @pl.when(i < 2)
+        def _():
+            weight_sums(1, xa1, rg, s, kept(s))
+
     def out_copy(i, s):
         return pltpu.make_async_copy(yc.at[s], y_h.at[net_of(i), s], ysem.at[s])
 
@@ -596,12 +606,9 @@
 
     def third_phase(i, s):
         kf = kept(s)
-
-        @pl.when(i > 0)
-        def _():
-            in_grad_copy(i, s).wait()
-
         total = rows_take(i, 2, s)
+        window(3, i, s)
+        spread(s, PBIAS, row(s, B3))
         s1, s2 = total[0:1], total[1:2] * row(s, R1)
         sc1, gain1, inverse, mean = row(s, SC1), row(s, G1), row(s, R1), row(s, MU1)
         grouped = group_rows(stack(gain1 * sc1 * s1, gain1 * sc1 * s2))
@@ -612,9 +619,8 @@
         spread(s, PDA, 0.5 * a)
         spread(s, PDB, b)
         spread(s, PDC, c)
-        spread(s, PBIAS, row(s, B3))
         dscale = gain1 * s2 + row(s, B2) * s1
-        here = sb.at[i, dp]
+        here = sb.at[i, place]
         here[1:2, 0:C] = here[1:2, 0:C] + sc1 * s2
         here[3:4, 0:C] = here[3:4, 0:C] + a * s1 + b * row(s, SUMH) + c * g.pixels
         here[4:5, 0:C] = here[4:5, 0:C] + sc1 * s1
@@ -626,7 +632,15 @@
             at = 8 + S + slot
             here[at : at + 1, 0 : 2 * C] = jnp.where(s == slot, modulation, here[at : at + 1, 0 : 2 * C])
 
+        def output():
+            for q in range(NP):
+                for rows in chunks():
+                    v = ybuf[rows, tile(q)] + prm[s, PBIAS, rows]
+                    v = (v + xc[s, rows, tile(q)].astype(F32)) * kf
+                    yc[s, rows, tile(q)] = v.astype(BF16)
+
         def hidden_grad(with_weights):
+            ybuf[...] = jnp.dot(wf[1], windows(xa1, s, False, False), preferred_element_type=F32)
             for n, qs in enumerate(quads()):
                 for rows in chunks():
                     pa, pb, pc = prm[s, PDA, rows], prm[s, PDB, rows], prm[s, PDC, rows]
@@ -641,27 +655,26 @@
                 if n == 0:
                     d = dub[s, :, tile(NP)] * prm[s, PDA] + hbuf[s, :, tile(NP)] * prm[s, PDB] + prm[s, PDC]
                     put_edges(xg, s, jnp.where(edge_ok, d, 0.0), None)
-            if with_weights:
-                o = jnp.dot(windows(xa1, s, False, False), pixels(rg, s), preferred_element_type=F32)
-                gacc[1] = gacc[1] + o * kf
-
-        def output(with_weights):
-            dub[s, :, 0:PX] = jnp.dot(wf[1], windows(xa1, s, False, False), preferred_element_type=F32)
-            for q in range(NP):
-                for rows in chunks():
-                    v = dub[s, rows, tile(q)] + prm[s, PBIAS, rows]
-                    v = (v + xc[s, rows, tile(q)].astype(F32)) * kf
-                    yc[s, rows, tile(q)] = v.astype(BF16)
-            if with_weights:
-                gacc[0] = gacc[0] + jnp.dot(windows(xa0, s, False, False), pixels(dhp, s), preferred_element_type=F32)
-
-        for piece in (hidden_grad, output):
-            pl.when(i < 2)(functools.partial(piece, True))
-            pl.when(i == 2)(functools.partial(piece, False))
+
+        @pl.when(i > 0)
+        def _():
+            in_grad_copy(i, s).wait()
+
+        @pl.when(i < 2)
+        def _():
+            hidden_grad(True)
+            output()
+            weight_sums(0, xa0, dhp, s, None)
+
+        @pl.when(i == 2)
+        def _():
+            hidden_grad(False)
+            output()
 
         out_copy(i, s).start()
 
     def fourth_phase(i, s):
+        window(4, i, s)
         clear(2)
         hbuf[s, :, 0:PX] = jnp.dot(wb[0], windows(xg, s, True, False), preferred_element_type=F32)
         for q in range(NP):
@@ -685,7 +698,7 @@
         spread(s, PA1, 0.5 * inverse * gain0)
         spread(s, PB1, b)
         spread(s, PMU1, -inverse * m1 - mean * b)
-        here = sb.at[i, dp]
+        here = sb.at[i, place]
         here[0:1, 0:C] = here[0:1, 0:C] + s4
         here[2:3, 0:C] = here[2:3, 0:C] + s3
         out_copy(i, s).wait()
@@ -699,30 +712,74 @@
         in_grad_copy(i, s).start()
 
 
-    final = list(range(5, g.stages + 1))
-    plan = {
-        (0, 3, S - 1): [(0, 0)],
-        (0, 4, S - 1): [(0, 1)],
-        (1, 2, 0): [(0, 2)],
-        (1, 3, 0): [(0, 3)],
-        (1, 3, S - 1): [(1, 0)],
-        (1, 4, S - 1): [(0, 4), (1, 1)],
-        (2, 1, S - 1): [(0, t) for t in final[:-1]],
-        (2, 2, 0): [(1, 2)],
-        (2, 2, S - 1): [(0, final[-1])],
-        (2, 3, 0): [(1, 3)],
-        (2, 5, S - 1): [(1, 4)] + [(1, t) for t in final],
+    last_slot = S - 1
+    plan = {}
+
+    def at(i, number, slot, action, *args):
+        plan.setdefault((i, number, slot), []).append(functools.partial(action, *args))
+
+    for m in range(2):
+        at(m, 2, last_slot, tick, m, 1, 0)
+        at(m, 3, 0, tick, m, 1, 1)
+        at(m, 3, last_slot, tick, m, 0, 0)
+        at(m, 4, last_slot, tick, m, 1, 2)
+        at(m, 4, last_slot, tick, m, 0, 1)
+        at(m + 1, 1, 0, tick, m, 1, 3)
+        at(m + 1, 1, last_slot, tick, m, 0, 2)
+        at(m + 1, 1, last_slot, small_start, m, 0)
+        at(m + 1, 2, last_slot, small_finish, m, 0)
+        at(m + 1, 2, last_slot, small_start, m, 1)
+        for t in range(4, g.bits + 1):
+            at(m + 1, 2, last_slot, tick, m, 1, t)
+        at(m + 1, 2, last_slot, tick, m, 0, 3)
+        at(m + 1, 3, last_slot, small_finish, m, 1)
+        at(m + 1, 3, last_slot, tick, m, 1, g.bits + 1)
+        for t in range(4, g.bits + 1):
+            at(m + 1, 3, last_slot, tick, m, 0, t)
+        for r in range(2, g.bits - 1):
+            at(m + 1, 3, last_slot, small_start, m, r)
+            if r < g.bits - 2:
+                at(m + 1, 3, last_slot, small_finish, m, r)
+        at(m + 1, 4, 0, tick, m, 1, g.stages)
+        at(m + 1, 5, last_slot, small_finish, m, g.bits - 2)
+        at(m + 1, 5, last_slot, tick, m, 0, g.bits + 1)
+        end = (m + 2, 1, 0) if m == 0 else (m + 1, 5, last_slot)
+        at(*end, tick, m, 0, g.stages)
+
+    def start_x(s):
+        return lambda i: halo_start(i, s, 0)
+
+    def start_gy(s):
+        return lambda i: halo_start(i, s, 1)
+
+    def start_weights(k, j):
+        return lambda i: weights_start(i, k, j)
+
+    sends = {
+        (2, 0): [start_x(0)],
+        (2, 1): [start_x(1)],
+        (3, 0): [start_weights(0, j) for j in range(TRIPLES)],
+        (3, S - 1): [start_weights(1, j) for j in range(TRIPLES)],
+        (4, 0): [start_gy(0)],
+        (4, 1): [start_gy(1)],
     }
+    def window(number, i, s):
+        for (where, slot), actions in sends.items():
+            if where == number:
+                @pl.when((i < 2) & (s == slot))
+                def _():
+                    for action in actions:
+                        action(i + 1)
 
     def slots(number, phase, i):
         def step(s, carry):
             phase(i, s)
-            for (at, where, slot), ticks in plan.items():
+            for (turn, where, slot), actions in plan.items():
                 if where == number:
-                    @pl.when((i == at) & (s == slot))
+                    @pl.when((i == turn) & (s == slot))
                     def _():
-                        for m, t in ticks:
-                            tick(m, t)
+                        for action in actions:
+                            action()
             return carry
 
         lax.fori_loop(0, S, step, 0)
@@ -739,12 +796,12 @@
     load_gy(0)
     fill = g.low_rows + g.high_rows
     pk[:, :, :, fill:, :] = jnp.zeros((2, 2, F, g.pack - fill, LANES), F32)
-    sb[:, dp] = jnp.zeros((3, 16, g.wide), F32)
+    sb[:, place] = jnp.zeros((3, 16, g.wide), F32)
     for n in range(g.nets):
         own = own_embedding(n)
         for i in range(3):
             if (2 * i) % g.nets == n:
-                sb[i, dp, 8 : 8 + S, 0 : g.ef] = own.astype(F32)
+                sb[i, place, 8 : 8 + S, 0 : g.ef] = own.astype(F32)
 
     @pl.when(me == 0)
     def _():
@@ -761,28 +818,51 @@
     for bits in partners:
         pl.semaphore_signal(barrier, inc=1, device_id={"dp": other(*bits)}, device_id_type=MESH)
     pl.semaphore_wait(barrier, F - 1 + len(partners))
-    halos_start(0, 0)
-    weights_start(0)
+    weight_local(0).start()
+    halo_start(0, 0, 0)
+    for j in range(TRIPLES):
+        weights_start(0, 0, j)
+    for s in range(1, S):
+        halo_start(0, s, 0)
+    for j in range(TRIPLES):
+        weights_start(0, 1, j)
+    for s in range(S):
+        halo_start(0, s, 1)
     slots(0, sums_phase, 0)
-    halos_start(0, 1)
+    weights_forward(0, 0)
+    weight_local(0).wait()
+    weights_take(0, 0)
+    weights_ready(0, 0)
+
+    def first_of_all(i, s):
+        first_phase(i, s)
+
+        @pl.when((i == 0) & (s == 0))
+        def _():
+            weights_forward(0, 1)
+            weights_take(0, 1)
+            weights_ready(0, 1)
+
+    def fourth_and_weights(i, s):
+        fourth_phase(i, s)
+
+        @pl.when((i < 2) & (s == 0))
+        def _():
+            for k in range(2):
+                weights_forward(i + 1, k)
 
     def network(i, carry):
         @pl.when(i < 2)
         def _():
             gacc[...] = jnp.zeros(gacc.shape, F32)
 
-        weights_forward(i)
-        weights_take(i)
-        weights_ready(i)
-        slots(1, first_phase, i)
+        slots(1, first_of_all, i)
         weights_sent(i)
 
         @pl.when(i < 2)
         def _():
             load_x(i + 1)
-            halos_start(i + 1, 0)
-            weights_start(i + 1)
-            halos_start(i + 1, 1)
+            weight_local(i + 1).start()
 
         slots(2, second_phase, i)
         slots(3, third_phase, i)
@@ -791,11 +871,15 @@
         def _():
             load_gy(i + 1)
 
-        slots(4, fourth_phase, i)
+        slots(4, fourth_and_weights, i)
 
         @pl.when(i < 2)
         def _():
             slots(0, sums_phase, i + 1)
+            weight_local(i + 1).wait()
+            for k in range(2):
+                weights_take(i + 1, k)
+                weights_ready(i + 1, k)
 
         slots(5, last_phase, i)
         return carry
@@ -810,8 +894,6 @@
             for e in range(4):
                 for df in range(1, F):
                     row_copy(i, e, s, df, me).wait_send()
-        for df in range(1, F):
-            weight_copy(i, df, me).wait_send()
         return carry
 
     lax.fori_loop(0, 3, drain, 0)
@@ -880,11 +962,11 @@
         pltpu.VMEM((2, chans, 9 * chans), BF16),
         pltpu.VMEM((2, 9 * chans, chans), F32),
         pltpu.VMEM((2, 2, fsdp, g.pack, LANES), F32),
-        pltpu.VMEM((2, fsdp, g.half, LANES), F32),
+        pltpu.VMEM((3 - g.split, 2, fsdp, g.half, LANES), F32),
         pltpu.VMEM((2, 3, fsdp, g.piece, LANES), F32),
-        pltpu.VMEM((2, fsdp - 1, g.piece, LANES), F32),
-        pltpu.VMEM((2, fsdp - 1, g.half, LANES), F32),
+        pltpu.VMEM((2, 2, fsdp - 1, g.piece, LANES), F32),
         pltpu.VMEM((2, g.bits - 3, g.piece, LANES), F32),
+        pltpu.VMEM((chans, g.px), F32),
         pltpu.VMEM((slots, chans, g.px), BF16),
         pltpu.VMEM((embed_rows, 2 * chans), F32),
         pltpu.VMEM((3, slots, fsdp, 16, chans), F32),
@@ -901,12 +983,12 @@
         dma((3, 4, slots, fsdp)),
         dma((3, 4, slots, fsdp)),
         dma((3,)),
-        dma((3, fsdp)),
-        dma((3, fsdp)),
-        dma((3, fsdp)),
-        dma((3, fsdp)),
-        dma((2, 2, g.stages, max(3, fsdp))),
-        dma((2, 2, g.stages, max(3, fsdp))),
+        dma((3, 2, 3, fsdp)),
+        dma((3, 2, 3, fsdp)),
+        dma((3, 2, fsdp)),
+        dma((3, 2, fsdp)),
+        dma((2, 2, g.stages, max(3, fsdp - 1))),
+        dma((2, 2, g.stages, max(3, fsdp - 1))),
         dma((2, g.bits + 2)),
         dma((2, g.bits + 2)),
         dma((2, 3)),

time: 183 us -> 155 us (0.85)
  Pallas kernels: 177 us -> 149 us
    pallas_call x1, Pallas kernels: 166 us -> 137 us  [on_device(): pl.pallas_call(functools.partial(kernel_body, g), out_shape=(channel_majo...]
where the time goes in v3:
time: 155 us; the launch traced here: 154 us
  Pallas kernels  149 us (96%)
  local copies, waits for them, and re-layouts  4.35 us (3%)
    pallas_call x1, Pallas kernels, on_device(): pl.pallas_call(functools.partial(kernel_body, g), out_shape=(channel_majo...  137 us
    pallas_call x1, Pallas kernels, on_device(): pl.pallas_call(functools.partial(place_body, g), grid=(nets * slots,), ou...  11.8 us
    unnamed x7, local copies, waits for them, and re-layouts  4.35 us

profile of v3, /device:TPU:0, one launch (start us, length us, event | category | flops | bytes accessed | tf_op | source)
XLA Modules:
  0.0 154.4 jit_solution(1568727032589290826)
XLA Ops:
  1.3 137.0 %shard_map.127 = (bf16[3,2,192,2048]{3,2,1,0:T(8,128)(2,1)}, bf16[3,2,192,2048]{3,2,1,0:T(8,128)(2,1)}, f32[2,2,1344,128]{3,2,1,0:T(8,128)}, f32[2,384,384]{2,1,0:T(8,128)}, f32[2,8,256]{2,1,0:T(8,128)}) custom-call(bf16[3,2,32,64,192]{4,3,2,1,0:T(8,128)(2,1)} %x_h.1, bf16[3,2,32,64,192]{4,3,2,1,0:T(8,128)(2,1)} %gy_h.1, ...), custom_call_target="tpu_custom_call" | custom-call | tf_op jit(solution)/shard_map/pallas_call | solution.py:1000
  138.2 0.0 copy-start
  138.3 1.8 %copy-done = f32[2,2,1344,128]{3,2,1,0:T(8,128)S(1)} copy-done((f32[2,2,1344,128]{3,2,1,0:T(8,128)S(1)}, f32[2,2,1344,128]{3,2,1,0:T(8,128)}, u32[]{:S(2)}) %copy-start) | copy-done | bytes 2752536
  140.0 0.0 copy-start.1
  140.0 1.3 copy-done.1
  141.3 0.0 copy-start.2
  141.3 0.7 copy-done.2
  142.0 11.8 %shard_map.128 = (bf16[3,2,32,64,192]{4,3,2,1,0:T(8,128)(2,1)}, bf16[3,2,32,64,192]{4,3,2,1,0:T(8,128)(2,1)}, f32[2,2,864,192]{3,2,1,0:T(8,128)}, f32[2,384,384]...) custom-call(bf16[3,2,192,2048]{3,2,1,0:T(8,128)(2,1)} %get-tuple-element.17.y_c, ...), custom_call_target="tpu_custom_call" | custom-call | tf_op jit(solution)/shard_map/pallas_call | solution.py:1027
  153.8 0.6 copy.14
Async XLA Ops:
  138.2 1.8 %copy-start = (f32[2,2,1344,128]{3,2,1,0:T(8,128)S(1)}, f32[2,2,1344,128]{3,2,1,0:T(8,128)}, u32[]{:S(2)}) copy-start(f32[2,2,1344,128]{3,2,1,0:T(8,128)} %get-tuple-element.19.packed) | copy-start | bytes 8257540
  140.0 1.3 copy-start.1
  141.3 0.7 copy-start.2

commit v4 on v3

--- a/solution.py
+++ b/solution.py
@@ -458,28 +458,30 @@
             gacc[k, rows] = gacc[k, rows] + (o if factor is None else o * factor)
 
 
-    def sums_phase(i, s):
+    def input_work(i, s):
         n = net_of(i)
-        pltpu.make_async_copy(x_h.at[n, s], rx.at[s], lx.at[s]).wait()
-
-        def step(h, carry):
-            a, b = carry
-            v = rx[s, h].astype(F32)
-            v = v.reshape(g.w // 8, 8, C)
-            return a + jnp.sum(v, axis=0), b + jnp.sum(v * v, axis=0)
-
-        zero = jnp.zeros((8, C), F32)
-        a, b = lax.fori_loop(0, R, step, (zero, zero), unroll=4)
+        clear(2)
+        for qs in quads():
+            for q in qs:
+                xc[i % 2, s, :, tile(q)] = pair(rx, s, q).T
+            for rows in chunks():
+                a0, a1 = acc[0, rows], acc[1, rows]
+                for q in qs:
+                    xf = xc[i % 2, s, rows, tile(q)].astype(F32)
+                    a0 = a0 + xf
+                    a1 = a1 + xf * xf
+                acc[0, rows], acc[1, rows] = a0, a1
         mod = jnp.dot(own_embedding(n).astype(BF16), aff[n], preferred_element_type=F32)
         which = lax.broadcasted_iota(jnp.int32, mod.shape, 0) == s
         mod = jnp.sum(jnp.where(which, mod, 0.0), axis=0, keepdims=True)
-        ex1[i, s, me, 0:8] = stack(
-            jnp.sum(a, axis=0, keepdims=True), jnp.sum(b, axis=0, keepdims=True), mod[:, 0:C], mod[:, C : 2 * C],
-        )
+        ex1[i, s, me, 0:8] = stack(total_row(0), total_row(1), mod[:, 0:C], mod[:, C : 2 * C])
         vectors = jnp.concatenate([gains[n], biases[n]], axis=0).astype(F32)
         vectors = jnp.concatenate([vectors, jnp.zeros((8, 2 * LANES - g.shard), F32)], axis=1)
         ex1[i, s, me, 8:16] = pltpu.roll(vectors, me * g.shard, 1)[:, 0:C]
         rows_start(i, 0, s)
+
+    def input_loaded(i, s):
+        pltpu.make_async_copy(x_h.at[net_of(i), s], rx.at[s], lx.at[s]).wait()
 
     def weights_ready(i, k):
         for tap in range(9):
@@ -495,11 +497,10 @@
         far = jnp.concatenate([hb[i % 2, s, t, 0, 0], hb[i % 2, s, t, 1, 1]], axis=0).T.astype(F32)
         return near, far
 
-    def first_phase(i, s):
-        kf = kept(s)
+    def gradient_loaded(i, s):
         pltpu.make_async_copy(gy_h.at[net_of(i), s], rg.at[s], lg.at[s]).wait()
-        halo_take(i, s, 0)
-        halo_take(i, s, 1)
+
+    def prepare(i, s):
         total = rows_take(i, 0, s)
         mean, inverse = moments(total[0:8])
         save(s, MU0, mean)
@@ -516,38 +517,25 @@
         spread(s, PB0, 0.5 * (total[10:11] - mean * scale))
         spread(s, PMU0, mean)
         spread(s, PBIAS, total[11:12])
-        clear(3)
 
         def act(xf, a, b):
             w = xf * a + b
             return w * jnp.tanh(w) + w
 
-        def body(qs):
-            for q in qs:
-                xc[s, :, tile(q)] = pair(rx, s, q).T
+        for n, qs in enumerate(quads()):
             for rows in chunks():
                 a, b = prm[s, PA0, rows], prm[s, PB0, rows]
                 for q in qs:
-                    put(xa0, s, rows, q + 1, act(xc[s, rows, tile(q)].astype(F32), a, b))
-
-        def edges():
-            near, far = edge_tiles(i, s, 0)
-            near = jnp.where(edge_ok, act(near, prm[s, PA0], prm[s, PB0]), 0.0)
-            far = jnp.where(edge_ok, act(far, prm[s, PA0], prm[s, PB0]), 0.0)
-            put_edges(xa0, s, near, far)
-
-        for n, qs in enumerate(quads()):
-            body(qs)
+                    put(xa0, s, rows, q + 1, act(xc[i % 2, s, rows, tile(q)].astype(F32), a, b))
             if n == 0:
-                edges()
-        hbuf[s] = jnp.dot(wf[0], windows(xa0, s, False, True), preferred_element_type=F32)
-        for q in range(NP + 1):
-            for rows in chunks():
-                h = hbuf[s, rows, tile(q)] + prm[s, PBIAS, rows]
-                hbuf[s, rows, tile(q)] = h
-                if q < NP:
-                    acc[0, rows] = acc[0, rows] + h
-                    acc[1, rows] = acc[1, rows] + h * h
+                near, far = edge_tiles(i, s, 0)
+                near = jnp.where(edge_ok, act(near, prm[s, PA0], prm[s, PB0]), 0.0)
+                far = jnp.where(edge_ok, act(far, prm[s, PA0], prm[s, PB0]), 0.0)
+                put_edges(xa0, s, near, far)
+
+    def prepare_gradient(i, s):
+        kf = kept(s)
+        acc[2] = jnp.zeros((C, LANES), F32)
         for qs in quads():
             for q in qs:
                 gc[s, :, tile(q)] = (pair(rg, s, q).T.astype(F32) * kf).astype(BF16)
@@ -558,10 +546,43 @@
                     a2 = a2 + gf
                     put(xg, s, rows, q + 1, gf)
                 acc[2, rows] = a2
-        near, far = edge_tiles(i, s, 1)
-        put_edges(xg, s, jnp.where(edge_ok, near, 0.0) * kf, jnp.where(edge_ok, far, 0.0) * kf)
-        ex2[i, 0, s, me] = stack(total_row(0), total_row(1), total_row(2))
+        save(s, SGY, total_row(2))
+
+    def first_phase(i, s):
+        kf = kept(s)
+
+        def gradient_edges():
+            near, far = edge_tiles(i, s, 1)
+            put_edges(xg, s, jnp.where(edge_ok, near, 0.0) * kf, jnp.where(edge_ok, far, 0.0) * kf)
+
+        def work(with_prepare):
+            if with_prepare:
+                gradient_loaded(i, s)
+                halo_take(i, s, 0)
+                halo_take(i, s, 1)
+                prepare(i, s)
+            clear(2)
+            hbuf[s] = jnp.dot(wf[0], windows(xa0, s, False, True), preferred_element_type=F32)
+            for q in range(NP + 1):
+                for rows in chunks():
+                    h = hbuf[s, rows, tile(q)] + prm[s, PBIAS, rows]
+                    hbuf[s, rows, tile(q)] = h
+                    if q < NP:
+                        acc[0, rows] = acc[0, rows] + h
+                        acc[1, rows] = acc[1, rows] + h * h
+            if with_prepare:
+                prepare_gradient(i, s)
+                gradient_edges()
+
+        pl.when(i == 0)(functools.partial(work, False))
+        pl.when(i > 0)(functools.partial(work, True))
+        ex2[i, 0, s, me] = stack(total_row(0), total_row(1), row(s, SGY))
         rows_start(i, 1, s)
+
+        @pl.when(i == 0)
+        def _():
+            halo_take(i, s, 1)
+            gradient_edges()
 
     def second_phase(i, s):
         total = rows_take(i, 1, s)
@@ -636,7 +657,7 @@
             for q in range(NP):
                 for rows in chunks():
                     v = ybuf[rows, tile(q)] + prm[s, PBIAS, rows]
-                    v = (v + xc[s, rows, tile(q)].astype(F32)) * kf
+                    v = (v + xc[i % 2, s, rows, tile(q)].astype(F32)) * kf
                     yc[s, rows, tile(q)] = v.astype(BF16)
 
         def hidden_grad(with_weights):
@@ -663,8 +684,10 @@
         @pl.when(i < 2)
         def _():
             hidden_grad(True)
+            input_loaded(i + 1, s)
+            weight_sums(0, xa0, dhp, s, None)
             output()
-            weight_sums(0, xa0, dhp, s, None)
+            input_work(i + 1, s)
 
         @pl.when(i == 2)
         def _():
@@ -674,12 +697,11 @@
         out_copy(i, s).start()
 
     def fourth_phase(i, s):
-        window(4, i, s)
         clear(2)
         hbuf[s, :, 0:PX] = jnp.dot(wb[0], windows(xg, s, True, False), preferred_element_type=F32)
         for q in range(NP):
             for rows in chunks():
-                xf = xc[s, rows, tile(q)].astype(F32)
+                xf = xc[i % 2, s, rows, tile(q)].astype(F32)
                 w = xf * prm[s, PA0, rows] + prm[s, PB0, rows]
                 d = hbuf[s, rows, tile(q)] * slope_twice(w, jnp.tanh(w))
                 hbuf[s, rows, tile(q)] = d
@@ -706,7 +728,7 @@
             for rows in chunks():
                 pa, pb, pc = prm[s, PA1, rows], prm[s, PB1, rows], prm[s, PMU1, rows]
                 for q in qs:
-                    xf = xc[s, rows, tile(q)].astype(F32)
+                    xf = xc[i % 2, s, rows, tile(q)].astype(F32)
                     v = hbuf[s, rows, tile(q)] * pa + xf * pb + pc + gc[s, rows, tile(q)].astype(F32)
                     yc[s, rows, tile(q)] = v.astype(BF16)
         in_grad_copy(i, s).start()
@@ -722,7 +744,7 @@
         at(m, 2, last_slot, tick, m, 1, 0)
         at(m, 3, 0, tick, m, 1, 1)
         at(m, 3, last_slot, tick, m, 0, 0)
-        at(m, 4, last_slot, tick, m, 1, 2)
+        at(m, 5, 0, tick, m, 1, 2)
         at(m, 4, last_slot, tick, m, 0, 1)
         at(m + 1, 1, 0, tick, m, 1, 3)
         at(m + 1, 1, last_slot, tick, m, 0, 2)
@@ -756,12 +778,10 @@
         return lambda i: weights_start(i, k, j)
 
     sends = {
-        (2, 0): [start_x(0)],
-        (2, 1): [start_x(1)],
+        (2, 0): [start_x(s) for s in range(S)],
+        (2, 1): [start_gy(s) for s in range(S)],
         (3, 0): [start_weights(0, j) for j in range(TRIPLES)],
         (3, S - 1): [start_weights(1, j) for j in range(TRIPLES)],
-        (4, 0): [start_gy(0)],
-        (4, 1): [start_gy(1)],
     }
     def window(number, i, s):
         for (where, slot), actions in sends.items():
@@ -819,16 +839,25 @@
         pl.semaphore_signal(barrier, inc=1, device_id={"dp": other(*bits)}, device_id_type=MESH)
     pl.semaphore_wait(barrier, F - 1 + len(partners))
     weight_local(0).start()
-    halo_start(0, 0, 0)
+    for s in range(S):
+        halo_start(0, s, 0)
+
+    def prepare_first(i, s):
+        gradient_loaded(i, s)
+        halo_take(i, s, 0)
+        prepare(i, s)
+        prepare_gradient(i, s)
+
+    for s in range(S):
+        input_loaded(0, s)
+    slots(0, input_work, 0)
     for j in range(TRIPLES):
         weights_start(0, 0, j)
-    for s in range(1, S):
-        halo_start(0, s, 0)
+    for s in range(S):
+        halo_start(0, s, 1)
     for j in range(TRIPLES):
         weights_start(0, 1, j)
-    for s in range(S):
-        halo_start(0, s, 1)
-    slots(0, sums_phase, 0)
+    slots(0, prepare_first, 0)
     weights_forward(0, 0)
     weight_local(0).wait()
     weights_take(0, 0)
@@ -837,7 +866,7 @@
     def first_of_all(i, s):
         first_phase(i, s)
 
-        @pl.when((i == 0) & (s == 0))
+        @pl.when((i == 0) & (s == S - 1))
         def _():
             weights_forward(0, 1)
             weights_take(0, 1)
@@ -875,7 +904,6 @@
 
         @pl.when(i < 2)
         def _():
-            slots(0, sums_phase, i + 1)
             weight_local(i + 1).wait()
             for k in range(2):
                 weights_take(i + 1, k)
@@ -906,22 +934,24 @@
 
 
 def place_body(g, y_c, dx_c, packed, affine, sums, y, dx, conv, affine_out, gain_out, bias_out):
-    for src, dst in ((y_c, y), (dx_c, dx)):
-        for q in range(g.np):
-            flat = src[0, 0, :, q * LANES : (q + 1) * LANES].T
-            dst[0, 0, q] = flat[0 : g.w]
-            dst[0, 0, q + g.np] = flat[g.w : 2 * g.w]
+    for s in range(g.s):
+        for src, dst in ((y_c, y), (dx_c, dx)):
+            for q in range(g.np):
+                flat = src[0, s, :, q * LANES : (q + 1) * LANES].T
+                dst[0, s, q] = flat[0 : g.w]
+                dst[0, s, q + g.np] = flat[g.w : 2 * g.w]
     step = pl.program_id(0)
 
-    @pl.when(step < 4)
+    @pl.when(step < 2)
     def _():
         split = g.low_rows - g.high_rows
         rest = g.c - LANES
-        conv[0, 0, :, 0:LANES] = packed[0, 0, 0 : g.low_rows, :]
-        conv[0, 0, 0 : g.high_rows, LANES : g.c] = packed[0, 0, g.low_rows : g.low_rows + g.high_rows, 0:rest]
-        conv[0, 0, g.high_rows : g.low_rows, LANES : g.c] = packed[
-            0, 0, g.low_rows : g.low_rows + split, CHUNK : CHUNK + rest
-        ]
+        for k in range(2):
+            conv[0, k, :, 0:LANES] = packed[0, k, 0 : g.low_rows, :]
+            conv[0, k, 0 : g.high_rows, LANES : g.c] = packed[0, k, g.low_rows : g.low_rows + g.high_rows, 0:rest]
+            conv[0, k, g.high_rows : g.low_rows, LANES : g.c] = packed[
+                0, k, g.low_rows : g.low_rows + split, CHUNK : CHUNK + rest
+            ]
 
     @pl.when(step < 2)
     def _():
@@ -949,7 +979,7 @@
         pltpu.VMEM((slots, rows, width, chans), BF16),
         pltpu.VMEM((slots, rows, width, chans), BF16),
         pltpu.VMEM((slots, rows, width, chans), BF16),
-        pltpu.VMEM((slots, chans, g.px), BF16),
+        pltpu.VMEM((2, slots, chans, g.px), BF16),
         pltpu.VMEM((slots, chans, g.px), BF16),
         pltpu.VMEM((slots, 3, chans, (g.np + 5) * LANES), BF16),
         pltpu.VMEM((slots, 3, chans, (g.np + 2) * LANES), BF16),
@@ -1015,18 +1045,18 @@
     )(block_input, out_cotangent, weights, affine_weight, embedding, gains, biases, counts)
 
     def by_slot(step):
-        return (step // slots, step % slots, 0, 0)
+        return (step, 0, 0, 0)
 
     def by_conv(step):
-        return (jnp.minimum(step, 3) // 2, jnp.minimum(step, 3) % 2, 0, 0)
+        return (jnp.minimum(step, 1), 0, 0, 0)
 
     def by_net(step):
         return (jnp.minimum(step, 1), 0, 0)
 
-    image = pl.BlockSpec((1, 1, rows, width, chans), lambda step: by_slot(step) + (0,))
+    image = pl.BlockSpec((1, slots, rows, width, chans), lambda step: by_slot(step) + (0,))
     block_output, input_grad, conv_grads, affine_grad, gain_grads, bias_grads = pl.pallas_call(
         functools.partial(place_body, g),
-        grid=(nets * slots,),
+        grid=(nets,),
         out_shape=(
             jax.ShapeDtypeStruct(block_input.shape, BF16),
             jax.ShapeDtypeStruct(block_input.shape, BF16),
@@ -1036,21 +1066,21 @@
             jax.ShapeDtypeStruct((2, 6, g.shard), F32),
         ),
         in_specs=[
-            pl.BlockSpec((1, 1, chans, g.px), by_slot),
-            pl.BlockSpec((1, 1, chans, g.px), by_slot),
-            pl.BlockSpec((1, 1, g.pack, LANES), by_conv),
+            pl.BlockSpec((1, slots, chans, g.px), by_slot),
+            pl.BlockSpec((1, slots, chans, g.px), by_slot),
+            pl.BlockSpec((1, 2, g.pack, LANES), by_conv),
             pl.BlockSpec((1, embed_rows, 2 * chans), by_net),
             vmem,
         ],
         out_specs=(
             image,
             image,
-            pl.BlockSpec((1, 1, g.low_rows, chans), by_conv),
+            pl.BlockSpec((1, 2, g.low_rows, chans), by_conv),
             pl.BlockSpec((1, embed_rows, 2 * chans), by_net),
             vmem,
             vmem,
         ),
-        compiler_params=pltpu.CompilerParams(vmem_limit_bytes=48 << 20),
+        compiler_params=pltpu.CompilerParams(vmem_limit_bytes=63 << 20),
     )(*main)
     conv_grads = conv_grads.reshape(2, 2, 3, 3, g.shard, chans)
     return block_output, input_grad, conv_grads, affine_grad, gain_grads, bias_grads

time: 155 us -> 143 us (0.923)
  Pallas kernels: 149 us -> 140 us
  local copies, waits for them, and re-layouts: 4.35 us -> 1.29 us
    pallas_call x1, Pallas kernels: 137 us -> 127 us  [on_device(): pl.pallas_call(functools.partial(kernel_body, g), out_shape=(channel_majo...]
    unnamed x7 -> x1, local copies, waits for them, and re-layouts: 4.35 us -> 1.29 us
where the time goes in v4:
time: 143 us; the launch traced here: 142 us
  Pallas kernels  140 us (98%)
    pallas_call x1, Pallas kernels, on_device(): pl.pallas_call(functools.partial(kernel_body, g), out_shape=(channel_majo...  127 us
    pallas_call x1, Pallas kernels, on_device(): pl.pallas_call(functools.partial(place_body, g), grid=(nets,), out_shape=...  12.7 us

profile of v4, /device:TPU:0, one launch (start us, length us, event | category | flops | bytes accessed | tf_op | source)
XLA Modules:
  0.0 142.3 jit_solution(5739190938896310687)
XLA Ops:
  1.3 127.0 %shard_map.127 = (bf16[3,2,192,2048]{3,2,1,0:T(8,128)(2,1)}, bf16[3,2,192,2048]{3,2,1,0:T(8,128)(2,1)}, f32[2,2,1344,128]{3,2,1,0:T(8,128)}, f32[2,384,384]{2,1,0:T(8,128)}, f32[2,8,256]{2,1,0:T(8,128)}) custom-call(bf16[3,2,32,64,192]{4,3,2,1,0:T(8,128)(2,1)} %x_h.1, bf16[3,2,32,64,192]{4,3,2,1,0:T(8,128)(2,1)} %gy_h.1, ...), custom_call_target="tpu_custom_call" | custom-call | tf_op jit(solution)/shard_map/pallas_call | solution.py:1030
  128.2 12.7 %shard_map.128 = (bf16[3,2,32,64,192]{4,3,2,1,0:T(8,128)(2,1)}, bf16[3,2,32,64,192]{4,3,2,1,0:T(8,128)(2,1)}, f32[2,2,864,192]{3,2,1,0:T(8,128)}, f32[2,384,384]...) custom-call(bf16[3,2,192,2048]{3,2,1,0:T(8,128)(2,1)} %get-tuple-element.17.y_c, ...), custom_call_target="tpu_custom_call" | custom-call | tf_op jit(solution)/shard_map/pallas_call | solution.py:1057
  141.0 1.3 copy.14

commit v5 on v4

--- a/solution.py
+++ b/solution.py
@@ -960,7 +960,8 @@
     @pl.when(step == 0)
     def _():
         gain_out[...] = sums[:, 0:2, 0 : g.shard]
-        bias_out[...] = sums[:, 2:8, 0 : g.shard]
+        for j in range(6):
+            bias_out[j] = sums[:, 2 + j, 0 : g.shard]
 
 
 def on_device(
@@ -1063,7 +1064,7 @@
             jax.ShapeDtypeStruct((2, 2, g.low_rows, chans), F32),
             jax.ShapeDtypeStruct((2, embed_rows, 2 * chans), F32),
             jax.ShapeDtypeStruct((2, 2, g.shard), F32),
-            jax.ShapeDtypeStruct((2, 6, g.shard), F32),
+            jax.ShapeDtypeStruct((6, 2, g.shard), F32),
         ),
         in_specs=[
             pl.BlockSpec((1, slots, chans, g.px), by_slot),
@@ -1083,7 +1084,7 @@
         compiler_params=pltpu.CompilerParams(vmem_limit_bytes=63 << 20),
     )(*main)
     conv_grads = conv_grads.reshape(2, 2, 3, 3, g.shard, chans)
-    return block_output, input_grad, conv_grads, affine_grad, gain_grads, bias_grads
+    return block_output, input_grad, conv_grads, affine_grad, gain_grads, bias_grads.transpose(1, 0, 2)
 
 
 def solution(mesh):

time: 143 us -> 141 us (0.986)
  no operation moved by 1% of the time
where the time goes in v5:
time: 141 us
  Pallas kernels  140 us (99%)
  between operations  1.45 us (1%)
    pallas_call x1, Pallas kernels, on_device(): pl.pallas_call(functools.partial(kernel_body, g), out_shape=(channel_majo...  127 us
    pallas_call x1, Pallas kernels, on_device(): pl.pallas_call(functools.partial(place_body, g), grid=(nets,), out_shape=...  12.7 us

profile of v5, /device:TPU:0, one launch (start us, length us, event | category | flops | bytes accessed | tf_op | source)
XLA Modules:
  0.0 141.2 jit_solution(16992394510664009426)
XLA Ops:
  1.3 127.0 %shard_map.127 = (bf16[3,2,192,2048]{3,2,1,0:T(8,128)(2,1)}, bf16[3,2,192,2048]{3,2,1,0:T(8,128)(2,1)}, f32[2,2,1344,128]{3,2,1,0:T(8,128)}, f32[2,384,384]{2,1,0:T(8,128)}, f32[2,8,256]{2,1,0:T(8,128)}) custom-call(bf16[3,2,32,64,192]{4,3,2,1,0:T(8,128)(2,1)} %x_h.1, bf16[3,2,32,64,192]{4,3,2,1,0:T(8,128)(2,1)} %gy_h.1, ...), custom_call_target="tpu_custom_call" | custom-call | tf_op jit(solution)/shard_map/pallas_call | solution.py:1031
  128.2 12.7 %shard_map.128 = (bf16[3,2,32,64,192]{4,3,2,1,0:T(8,128)(2,1)}, bf16[3,2,32,64,192]{4,3,2,1,0:T(8,128)(2,1)}, f32[2,2,864,192]{3,2,1,0:T(8,128)}, f32[2,384,384]...) custom-call(bf16[3,2,192,2048]{3,2,1,0:T(8,128)(2,1)} %get-tuple-element.17.y_c, ...), custom_call_target="tpu_custom_call" | custom-call | tf_op jit(solution)/shard_map/pallas_call | solution.py:1058
